TPU v7x, 256 devices: a whole 4x4x8 slice. The times are simulated.
256 devices in a mesh: grp: 4 (over y), sub: 64 (over x, z, core).
Axes of the slice: x: 4, y: 4, z: 8, core: 2. Of those that a mesh axis runs over, the one named last changes fastest.
Arguments:
- cotangent: float32 [2, 32, 512, 128], P(None, 'grp', 'sub'), may hold values from -6 to 6
- head: float32 [32, 512, 128], P('grp', 'sub'), may hold values from -6 to 6
- materials: int32 [32, 512, 128], P('grp', 'sub'), may hold values from 0 to 7
- flags: int32 [3, 32, 512, 128], P(None, 'grp', 'sub'), may hold values 0 or 1
- perm_table: float32 [8], replicated, may hold values from 0.3 to 3
- poro_table: float32 [8], replicated, may hold values from 0.1 to 0.45
Outputs:
- adjoint: float32 [2, 32, 512, 128], P(None, 'grp', 'sub')
All inputs are finite; a program needn't handle non-finite values. No bound on the sum of `flags` on one device may be relied on, other than what follows from the above.
Results may differ from a plain program's by a relative error of at most 0.0003.
Values sent between devices are 32-bit elements; how exact they have to be, the bound alone decides.
A program may use at most 64 MiB of HBM per device.

v0:
```python
import functools

import jax
import jax.numpy as jnp
from jax import lax
from jax.experimental import pallas as pl
from jax.experimental.pallas import tpu as pltpu
from jax.sharding import PartitionSpec as P

CX = 8
AGG = 4
ITERS = 4
DISP = 0.2
CPL_P = 0.5
CPL_S = 0.3
OMEGA = 0.7
OMEGA_C = 0.7
THETA = 0.5

PITCH = 12
BASE = 8
ROWS = 160
LANES = 128
MESH = pl.DeviceIdType.MESH

SIDES = [(-1, 0), (1, 0), (0, -1), (0, 1), (-1, -1), (-1, 1), (1, -1), (1, 1)]
NEAR = [-1, 1, -2, 2]

MAT, HEAD, F0, F1, F2, COT = 0, 1, 2, 3, 4, 5
TX, TXM, TY, TYM, TZ, TZM, SX, SXM, SY, SYM, SZ, SZM, BPP, BPC, BCP, BCC, IPP, IPC, ICP, ICC = range(20)
N_COEF = 20
N_CBLK = 13
C_ROWS = 56


def row(x, y):
    return BASE + (x + 2) * PITCH + y + 2


def rows(x, y, count=8):
    return pl.ds(row(x, y), count)


def column(y):
    return pl.ds(row(0, y), 8, stride=PITCH)


def setup_slots(low, along):
    if low:
        pairs = [(MAT, -2), (MAT, -1), (HEAD, -2), (HEAD, -1), (along, -2)]
        one = -1
    else:
        pairs = [(MAT, 8), (MAT, 9), (HEAD, 8), (HEAD, 9)]
        one = 8
    return pairs + [(field, one) for field in (F0, F1, F2, COT, COT + 1)]


def field_slots(low):
    return [(f, layer) for f in (0, 1) for layer in ((-2, -1) if low else (8, 9))]


def slots_of(side, setup):
    dx, dy = side
    if dx != 0:
        return setup_slots(dx < 0, F0) if setup else field_slots(dx < 0)
    return setup_slots(dy < 0, F1) if setup else field_slots(dy < 0)


def pack(side, setup, src, dst, lead):
    dx, dy = side
    for slot, (field, layer) in enumerate(slots_of(side, setup)):
        if dy == 0:
            dst[lead + (pl.ds(8 * slot, 8),)] = src[field, rows(layer % 8, 0), :]
        elif dx == 0:
            dst[lead + (pl.ds(8 * slot, 8),)] = src[field, column(layer % 8), :]
        else:
            dst[lead + (pl.ds(2 * slot, 2),)] = src[field, rows(layer % 8, 6 if dy < 0 else 0, 2), :]


def unpack(side, setup, src, lead, dst, valid):
    dx, dy = side

    def seen(field, value):
        return jnp.where(valid, value, -1.0) if setup and field == MAT else value

    for slot, (field, layer) in enumerate(slots_of(side, setup)):
        if dy == 0:
            dst[field, rows(layer, 0), :] = seen(field, src[lead + (pl.ds(8 * slot, 8),)])
        elif dx == 0:
            dst[field, column(layer), :] = seen(field, src[lead + (pl.ds(8 * slot, 8),)])
        else:
            dst[field, rows(layer, -2 if dy < 0 else 8, 2), :] = seen(field, src[lead + (pl.ds(2 * slot, 2),)])


def next_lane(value, by=1):
    return pltpu.roll(value, LANES - by, 1)


def last_lane(value, by=1):
    return pltpu.roll(value, by, 1)


def lane_sum(value):
    lane = lax.broadcasted_iota(jnp.int32, value.shape, 1)
    total = value + next_lane(value)
    total = total + next_lane(total, 2)
    total = jnp.where(lane % AGG == 0, total, 0.0)
    total = total + last_lane(total)
    return total + last_lane(total, 2)


def four_sum(value):
    total = value + pltpu.roll(value, 7, 0)
    return total + pltpu.roll(total, 6, 0)


def couple(co, field, lo, n):
    here = pl.ds(lo, n)
    out = []
    for f, first in ((0, TX), (1, SX)):
        mid = field[f, here, :]
        total = co[first, here, :] * field[f, pl.ds(lo + PITCH, n), :]
        total = total + co[first + 1, here, :] * field[f, pl.ds(lo - PITCH, n), :]
        total = total + co[first + 2, here, :] * field[f, pl.ds(lo + 1, n), :]
        total = total + co[first + 3, here, :] * field[f, pl.ds(lo - 1, n), :]
        total = total + co[first + 4, here, :] * next_lane(mid)
        total = total + co[first + 5, here, :] * last_lane(mid)
        out += [mid, total]
    return out


def kernel(
    n_grp,
    n_sub,
    cot_ref,
    head_ref,
    mat_ref,
    flag_ref,
    perm_tab,
    poro_tab,
    out_ref,
    ext,
    perm,
    poro,
    mask,
    face,
    co,
    adj,
    res,
    grd,
    mid,
    fin,
    ssend,
    srecv,
    hsend,
    hrecv,
    ksend,
    krecv,
    cagg,
    cco,
    csend,
    crecv,
    cres,
    s_send,
    s_recv,
    h_send,
    h_recv,
    k_send,
    k_recv,
    c_send,
    c_recv,
):
    g = lax.axis_index("grp")
    s = lax.axis_index("sub")

    def device(dx, dy):
        return {"grp": lax.rem(g + dx + n_grp, n_grp), "sub": lax.rem(s + dy + n_sub, n_sub)}

    barrier = pltpu.get_barrier_semaphore()
    partners = SIDES + [(0, -2), (0, 2)]
    for dx, dy in partners:
        pl.semaphore_signal(barrier, inc=1, device_id=device(dx, dy), device_id_type=MESH)

    zero_rows = jnp.zeros((ROWS, LANES), jnp.float32)
    ext[MAT] = zero_rows - 1.0
    for f in range(1, 7):
        ext[f] = zero_rows
    mask[...] = zero_rows
    for f in range(2):
        adj[f] = zero_rows
        grd[f] = zero_rows
        mid[f] = zero_rows
    for x in range(8):
        ext[MAT, rows(x, 0), :] = mat_ref[x].astype(jnp.float32)
        ext[HEAD, rows(x, 0), :] = head_ref[x]
        for d in range(3):
            ext[F0 + d, rows(x, 0), :] = flag_ref[d, x].astype(jnp.float32)
        for f in range(2):
            ext[COT + f, rows(x, 0), :] = cot_ref[f, x]
    for i, side in enumerate(SIDES):
        pack(side, True, ext, ssend, (i,))
    for x in range(-1, 9):
        mask[rows(x, -1, 10), :] = jnp.ones((10, LANES), jnp.float32)

    def exchange(i, setup, k):
        dx, dy = SIDES[i]
        count = len(slots_of((dx, dy), setup)) * (2 if dx != 0 and dy != 0 else 8)
        part = pl.ds(0, -(-count // 8) * 8)
        if setup:
            refs = (ssend.at[i, part], srecv.at[i, part], s_send.at[i], s_recv.at[i])
        else:
            refs = (hsend.at[k, i, part], hrecv.at[k, i, part], h_send.at[k, i], h_recv.at[k, i])
        return pltpu.make_async_remote_copy(*refs, device_id=device(-dx, -dy), device_id_type=MESH)

    def coarse_copy(j, k):
        return pltpu.make_async_remote_copy(
            csend.at[k], crecv.at[k, j], c_send.at[k, j], c_recv.at[k, j], device_id=device(0, -NEAR[j]), device_id_type=MESH
        )

    def coef_copy(j):
        return pltpu.make_async_remote_copy(
            ksend, krecv.at[j], k_send.at[j], k_recv.at[j], device_id=device(0, -NEAR[j]), device_id_type=MESH
        )

    pl.semaphore_wait(barrier, len(partners))
    for i in range(8):
        exchange(i, True, 0).start()

    def send_coarse(k, src, at):
        for f in range(2):
            for cx in range(2):
                total = src[at + f, rows(4 * cx, 0), :]
                for x in range(4 * cx + 1, 4 * cx + 4):
                    total = total + src[at + f, rows(x, 0), :]
                total = four_sum(total)
                first = 4 * f + 2 * cx
                cagg[pl.ds(first, 1), :] = total[0:1]
                cagg[pl.ds(first + 1, 1), :] = total[4:5]
        csend[k] = lane_sum(cagg[pl.ds(0, 8), :])
        for j in range(4):
            coarse_copy(j, k).start()

    send_coarse(0, ext, COT)

    for i, (dx, dy) in enumerate(SIDES):
        exchange(i, True, 0).wait_recv()
        fits = None
        for there, count, step in ((g, n_grp, dx), (s, n_sub, dy)):
            if step != 0:
                one = (there > 0) if step < 0 else (there < count - 1)
                fits = one if fits is None else jnp.logical_and(fits, one)
        unpack((dx, dy), True, srecv, (i,), ext, fits)

    for lo in range(0, ROWS, 32):
        here = pl.ds(lo, 32)
        mats = ext[MAT, here, :]
        perm_here = jnp.zeros_like(mats)
        poro_here = jnp.zeros_like(mats)
        for level in range(perm_tab.shape[0]):
            same = mats == float(level)
            perm_here = jnp.where(same, perm_tab[level], perm_here)
            poro_here = jnp.where(same, poro_tab[level], poro_here)
        perm[here, :] = perm_here
        poro[here, :] = poro_here

    for lo in range(0, 144, 24):
        here = pl.ds(lo, 24)
        perm_here, head_here = perm[here, :], ext[HEAD, here, :]
        lane = lax.broadcasted_iota(jnp.int32, (24, LANES), 1)
        for d in range(3):
            if d < 2:
                there = pl.ds(lo + (PITCH, 1)[d], 24)
                perm_next, head_next = perm[there, :], ext[HEAD, there, :]
            else:
                perm_next = jnp.where(lane == LANES - 1, 0.0, next_lane(perm_here))
                head_next = jnp.where(lane == LANES - 1, 0.0, next_lane(head_here))
            both = perm_here + perm_next
            trans = 2.0 * perm_here * perm_next / jnp.where(both > 0.0, both, 1.0)
            flux = trans * (0.5 + jnp.abs(head_here - head_next))
            upwind = ext[F0 + d, here, :]
            face[3 * d, here, :] = trans
            face[3 * d + 1, here, :] = upwind * flux
            face[3 * d + 2, here, :] = (1.0 - upwind) * flux

    for lo in range(16, 144, 16):
        here = pl.ds(lo, 16)
        total = jnp.zeros((16, LANES), jnp.float32)
        out = total
        for d in range(3):
            trans, upper, lower = (face[3 * d + m, here, :] for m in range(3))
            if d < 2:
                back = pl.ds(lo - (PITCH, 1)[d], 16)
                trans_m, lower_m = face[3 * d, back, :], face[3 * d + 2, back, :]
            else:
                trans_m, lower_m = last_lane(trans), last_lane(lower)
            co[TX + 2 * d, here, :] = trans
            co[TX + 2 * d + 1, here, :] = trans_m
            co[SX + 2 * d, here, :] = DISP * trans + upper
            co[SX + 2 * d + 1, here, :] = DISP * trans_m + lower_m
            total = total + trans + trans_m
            out = out + upper + lower_m
        store = poro[here, :]
        bpp, bpc, bcp, bcc = store + total, -CPL_S * out, CPL_P * store, store + DISP * total + out
        inside = jnp.logical_and(store > 0.0, mask[here, :] > 0.0)
        determ = jnp.where(inside, bpp * bcc - bpc * bcp, 1.0)
        scale = jnp.where(inside, OMEGA / determ, 0.0)
        for at, value in (
            (BPP, bpp), (BPC, bpc), (BCP, bcp), (BCC, bcc),
            (IPP, bcc * scale), (IPC, -bpc * scale), (ICP, -bcp * scale), (ICC, bpp * scale),
        ):
            co[at, here, :] = value

    def put(block, cx, cy, value):
        cagg[pl.ds(4 * block + 2 * cx + cy, 1), :] = value

    lane = lax.broadcasted_iota(jnp.int32, (8, LANES), 1)
    for cx in range(2):
        xs = range(4 * cx, 4 * cx + 4)
        store = poro[rows(4 * cx, 0), :]
        out = co[BPC, rows(4 * cx, 0), :]
        zs = [face[6 + m, rows(4 * cx, 0), :] for m in range(3)]
        for x in xs[1:]:
            store = store + poro[rows(x, 0), :]
            out = out + co[BPC, rows(x, 0), :]
            zs = [zs[m] + face[6 + m, rows(x, 0), :] for m in range(3)]
        zs = [jnp.where(lane % AGG == AGG - 1, z, 0.0) for z in zs]
        for block, value in ((0, store), (1, out), (12, zs[0]), (13, zs[1]), (14, zs[2])):
            value = four_sum(value)
            put(block, cx, 0, value[0:1])
            put(block, cx, 1, value[4:5])
    for d in range(2):
        first = 2 + 5 * d
        for member, ahead, behind in ((0, 0, 1), (1, 2, None), (2, 3, 4)):
            for place, edge in enumerate((-1, 3, 7)):
                if d == 0:
                    value = four_sum(face[member, rows(edge, 0), :])
                else:
                    value = four_sum(face[3 + member, column(edge), :])
                for other in range(2):
                    piece = value[4 * other : 4 * other + 1]
                    if place > 0:
                        cell = (place - 1, other) if d == 0 else (other, place - 1)
                        put(first + ahead, *cell, piece)
                    if place < 2 and behind is not None:
                        cell = (place, other) if d == 0 else (other, place)
                        put(first + behind, *cell, piece)
    cagg[pl.ds(60, 4), :] = jnp.zeros((4, LANES), jnp.float32)
    cagg[...] = lane_sum(cagg[...])

    def block(b):
        return cagg[pl.ds(4 * b, 4), :]

    store, cpc = block(0), block(1)
    t_z, a_z, b_z = block(12), block(13), block(14)
    edge_sum = block(2) + block(3) + block(7) + block(8) + t_z + last_lane(t_z, AGG)
    edge_out = block(4) + block(6) + block(9) + block(11) + a_z + last_lane(b_z, AGG)
    cpp, ccp, ccc = store + edge_sum, CPL_P * store, store + DISP * edge_sum + edge_out
    scale = OMEGA_C / (cpp * ccc - cpc * ccp)
    t_x, t_y = block(2), block(7)
    for b, value in enumerate((
        ccc * scale, -cpc * scale, -ccp * scale, cpp * scale,
        t_y, DISP * t_y + block(9), DISP * t_y + block(10),
        t_z, DISP * t_z + a_z, DISP * t_z + b_z,
        t_x, DISP * t_x + block(4), DISP * t_x + block(5),
    )):
        ksend[pl.ds(4 * b, 4), :] = value
    ksend[pl.ds(52, 4), :] = jnp.zeros((4, LANES), jnp.float32)
    for j in range(4):
        coef_copy(j).start()

    def spread(count, own, recv, dst):
        for item in range(count):
            dst(item, pl.ds(3, 2), own(pl.ds(2 * item, 2)))
            dst(item, pl.ds(1, 2), recv(0, pl.ds(2 * item, 2)))
            dst(item, pl.ds(5, 2), recv(1, pl.ds(2 * item, 2)))
            dst(item, pl.ds(0, 1), recv(2, pl.ds(2 * item + 1, 1)))
            dst(item, pl.ds(7, 1), recv(3, pl.ds(2 * item, 1)))

    def fine_solve(src, at):
        for lo in range(16, 144, 32):
            here = pl.ds(lo, 32)
            r_p, r_c = src[at, here, :], src[at + 1, here, :]
            grd[0, here, :] = co[IPP, here, :] * r_p + co[IPC, here, :] * r_c
            grd[1, here, :] = co[ICP, here, :] * r_p + co[ICC, here, :] * r_c
        for lo in range(16, 144, 16):
            here = pl.ds(lo, 16)
            z_p, s_p, z_c, s_c = couple(co, grd, lo, 16)
            mid[0, here, :] = (2.0 - OMEGA) * z_p + co[IPP, here, :] * s_p + co[IPC, here, :] * s_c
            mid[1, here, :] = (2.0 - OMEGA) * z_c + co[ICP, here, :] * s_p + co[ICC, here, :] * s_c
        for lo in range(32, 128, 16):
            here = pl.ds(lo, 16)
            z_p, s_p, z_c, s_c = couple(co, mid, lo, 16)
            fin[0, here, :] = (1.0 - OMEGA) * z_p + grd[0, here, :] + co[IPP, here, :] * s_p + co[IPC, here, :] * s_c
            fin[1, here, :] = (1.0 - OMEGA) * z_c + grd[1, here, :] + co[ICP, here, :] * s_p + co[ICC, here, :] * s_c

    def coarse_solve(k):
        for j in range(4):
            coarse_copy(j, k).wait_recv()

        def dst(item, where, value):
            cres[item, where, :] = value

        spread(4, lambda part: csend[k, part, :], lambda j, part: crecv[k, j, part, :], dst)
        ipp, ipc, icp, icc = ([cco[b, cx] for cx in range(2)] for b in range(4))
        t_y, a_y, b_y, t_z, a_z, b_z = ([cco[b, cx] for cx in range(2)] for b in range(4, 10))
        t_x, a_x, b_x = (cco[b, 0] for b in range(10, 13))
        ahead = {0: (t_y, t_z), 1: (a_y, a_z)}
        behind = {
            0: ([pltpu.roll(v, 1, 0) for v in t_y], [last_lane(v, AGG) for v in t_z]),
            1: ([pltpu.roll(v, 1, 0) for v in b_y], [last_lane(v, AGG) for v in b_z]),
        }
        across = {0: (t_x, t_x), 1: (a_x, b_x)}
        r = [[cres[2 * f + cx] for cx in range(2)] for f in range(2)]
        base = [
            [ipp[cx] * r[0][cx] + ipc[cx] * r[1][cx] for cx in range(2)],
            [icp[cx] * r[0][cx] + icc[cx] * r[1][cx] for cx in range(2)],
        ]
        z = base
        for sweep in range(3):
            acc = [[None] * 2 for f in range(2)]
            for f in range(2):
                for cx in range(2):
                    v = z[f][cx]
                    total = across[f][cx] * z[f][1 - cx]
                    total = total + ahead[f][0][cx] * pltpu.roll(v, 7, 0)
                    total = total + behind[f][0][cx] * pltpu.roll(v, 1, 0)
                    total = total + ahead[f][1][cx] * next_lane(v, AGG)
                    acc[f][cx] = total + behind[f][1][cx] * last_lane(v, AGG)
            z = [
                [(1.0 - OMEGA_C) * z[0][cx] + base[0][cx] + ipp[cx] * acc[0][cx] + ipc[cx] * acc[1][cx] for cx in range(2)],
                [(1.0 - OMEGA_C) * z[1][cx] + base[1][cx] + icp[cx] * acc[0][cx] + icc[cx] * acc[1][cx] for cx in range(2)],
            ]
        upper = lax.broadcasted_iota(jnp.int32, (8, LANES), 0) < AGG
        return [
            [
                jnp.where(upper, jnp.broadcast_to(v[3:4], (8, LANES)), jnp.broadcast_to(v[4:5], (8, LANES)))
                for v in z[f]
            ]
            for f in range(2)
        ]

    def update(k, last):
        grown = coarse_solve(k)
        for f in range(2):
            for x in range(8):
                here = rows(x, 0)
                new = adj[f, here, :] + THETA * (fin[f, here, :] + grown[f][x // 4])
                if last:
                    out_ref[f, x] = new
                else:
                    adj[f, here, :] = new

    def refresh(k):
        for i, side in enumerate(SIDES):
            pack(side, False, adj, hsend, (k, i))
            exchange(i, False, k).start()
        for i, side in enumerate(SIDES):
            exchange(i, False, k).wait_recv()
            unpack(side, False, hrecv, (k, i), adj, None)
        for lo in range(16, 144, 16):
            here = pl.ds(lo, 16)
            z_p, s_p, z_c, s_c = couple(co, adj, lo, 16)
            res[0, here, :] = ext[COT, here, :] + s_p - co[BPP, here, :] * z_p - co[BPC, here, :] * z_c
            res[1, here, :] = ext[COT + 1, here, :] + s_c - co[BCP, here, :] * z_p - co[BCC, here, :] * z_c

    fine_solve(ext, COT)

    def coef_dst(item, where, value):
        cco[item // 2, item % 2, where, :] = value

    for j in range(4):
        coef_copy(j).wait_recv()
    spread(2 * N_CBLK, lambda part: ksend[part, :], lambda j, part: krecv[j, part, :], coef_dst)
    update(0, False)
    refresh(0)

    def step(k, carry):
        send_coarse(k, res, 0)
        fine_solve(res, 0)
        update(k, False)
        refresh(k)
        return carry

    lax.fori_loop(1, ITERS - 1, step, 0)
    send_coarse(ITERS - 1, res, 0)
    fine_solve(res, 0)
    update(ITERS - 1, True)

    for i in range(8):
        exchange(i, True, 0).wait_send()
        for k in range(ITERS - 1):
            exchange(i, False, k).wait_send()
    for j in range(4):
        coef_copy(j).wait_send()
        for k in range(ITERS):
            coarse_copy(j, k).wait_send()


def solution(mesh):
    n_grp, n_sub = mesh.shape["grp"], mesh.shape["sub"]

    def local(cotangent, head, materials, flags, perm_table, poro_table):
        def tile(*shape):
            return pltpu.VMEM(shape + (LANES,), jnp.float32)

        dma = pltpu.SemaphoreType.DMA
        vmem = pl.BlockSpec(memory_space=pltpu.VMEM)
        smem = pl.BlockSpec(memory_space=pltpu.SMEM)
        return pl.pallas_call(
            functools.partial(kernel, n_grp, n_sub),
            out_shape=jax.ShapeDtypeStruct(cotangent.shape, jnp.float32),
            in_specs=[vmem] * 4 + [smem] * 2,
            out_specs=vmem,
            scratch_shapes=[
                tile(7, ROWS),
                tile(ROWS),
                tile(ROWS),
                tile(ROWS),
                tile(9, ROWS),
                tile(N_COEF, ROWS),
                tile(2, ROWS),
                tile(2, ROWS),
                tile(2, ROWS),
                tile(2, ROWS),
                tile(2, ROWS),
                tile(8, 80),
                tile(8, 80),
                tile(ITERS - 1, 8, 32),
                tile(ITERS - 1, 8, 32),
                tile(C_ROWS),
                tile(4, C_ROWS),
                tile(64),
                tile(N_CBLK, 2, 8),
                tile(ITERS, 8),
                tile(ITERS, 4, 8),
                tile(4, 8),
                dma((8,)),
                dma((8,)),
                dma((ITERS - 1, 8)),
                dma((ITERS - 1, 8)),
                dma((4,)),
                dma((4,)),
                dma((ITERS, 4)),
                dma((ITERS, 4)),
            ],
            compiler_params=pltpu.CompilerParams(
                collective_id=0, has_side_effects=True, vmem_limit_bytes=32 * 1024 * 1024
            ),
        )(cotangent, head, materials, flags, perm_table, poro_table)

    return jax.shard_map(
        local,
        mesh=mesh,
        in_specs=(
            P(None, "grp", "sub", None),
            P("grp", "sub", None),
            P("grp", "sub", None),
            P(None, "grp", "sub", None),
            P(),
            P(),
        ),
        out_specs=P(None, "grp", "sub", None),
        check_vma=False,
    )
```

profile of v0, /device:TPU:1, one launch (start us, length us, event | category | flops | bytes accessed | tf_op | source)
XLA Modules:
  0.0 57.1 jit_solution(18063306992823767186)
XLA Ops:
  0.0 0.0 copy-start
  0.0 0.9 %copy-done = s32[3,8,8,128]{3,2,1,0:T(8,128)S(1)} copy-done((s32[3,8,8,128]{3,2,1,0:T(8,128)S(1)}, s32[3,8,8,128]{3,2,1,0:T(8,128)}, u32[]{:S(2)}) %copy-start) | copy-done | bytes 98328
  0.9 0.0 copy-start.1
  0.9 0.8 %copy-done.1 = f32[2,8,8,128]{3,2,1,0:T(8,128)S(1)} copy-done((f32[2,8,8,128]{3,2,1,0:T(8,128)S(1)}, f32[2,8,8,128]{3,2,1,0:T(8,128)}, u32[]{:S(2)}) %copy-start.1) | copy-done | bytes 65560
  1.7 0.0 copy-start.2
  1.7 0.8 %copy-done.2 = f32[8,8,128]{2,1,0:T(8,128)S(1)} copy-done((f32[8,8,128]{2,1,0:T(8,128)S(1)}, f32[8,8,128]{2,1,0:T(8,128)}, u32[]{:S(2)}) %copy-start.2) | copy-done | bytes 32792
  2.5 0.0 copy-start.3
  2.5 0.8 %copy-done.3 = s32[8,8,128]{2,1,0:T(8,128)S(1)} copy-done((s32[8,8,128]{2,1,0:T(8,128)S(1)}, s32[8,8,128]{2,1,0:T(8,128)}, u32[]{:S(2)}) %copy-start.3) | copy-done | bytes 32792
  3.3 0.0 copy-start.4
  3.3 0.7 %copy-done.4 = f32[8]{0:T(128)S(1)} copy-done((f32[8]{0:T(128)S(1)}, f32[8]{0:T(128)}, u32[]{:S(2)}) %copy-start.4) | copy-done | bytes 56
  3.9 0.0 copy-start.5
  3.9 0.7 %copy-done.5 = f32[8]{0:T(128)S(1)} copy-done((f32[8]{0:T(128)S(1)}, f32[8]{0:T(128)}, u32[]{:S(2)}) %copy-start.5) | copy-done | bytes 56
  4.6 51.9 %shard_map.64 = f32[2,8,8,128]{3,2,1,0:T(8,128)S(1)} custom-call(f32[2,8,8,128]{3,2,1,0:T(8,128)S(1)} %copy-done.1, f32[8,8,128]{2,1,0:T(8,128)S(1)} %copy-done.2, s32[8,8,128]{2,1,0:T(8,128)S(1)} %copy-done.3, s32[3,8,8,128]{3,2,1,0:T(8,128)S(1)} %copy-done, f32[8]{0:T(128)S(1)} %copy-done.4, f32[8]{0:T(128)S(1)} %copy-done.5), custom_call_target="tpu_custom_call" | custom-call | tf_op jit(solution)/shard_map/pallas_call | solution.py:509
  56.5 0.6 %copy.8 = f32[2,8,8,128]{3,2,1,0:T(8,128)} copy(f32[2,8,8,128]{3,2,1,0:T(8,128)S(1)} %shard_map.64) | data formatting | bytes 131072
Async XLA Ops:
  0.0 0.9 %copy-start = (s32[3,8,8,128]{3,2,1,0:T(8,128)S(1)}, s32[3,8,8,128]{3,2,1,0:T(8,128)}, u32[]{:S(2)}) copy-start(s32[3,8,8,128]{3,2,1,0:T(8,128)} %flag_ref.1) | copy-start | bytes 294916
  0.9 0.8 %copy-start.1 = (f32[2,8,8,128]{3,2,1,0:T(8,128)S(1)}, f32[2,8,8,128]{3,2,1,0:T(8,128)}, u32[]{:S(2)}) copy-start(f32[2,8,8,128]{3,2,1,0:T(8,128)} %cot_ref.1) | copy-start | bytes 196612
  1.7 0.8 %copy-start.2 = (f32[8,8,128]{2,1,0:T(8,128)S(1)}, f32[8,8,128]{2,1,0:T(8,128)}, u32[]{:S(2)}) copy-start(f32[8,8,128]{2,1,0:T(8,128)} %head_ref.1) | copy-start | bytes 98308
  2.5 0.8 %copy-start.3 = (s32[8,8,128]{2,1,0:T(8,128)S(1)}, s32[8,8,128]{2,1,0:T(8,128)}, u32[]{:S(2)}) copy-start(s32[8,8,128]{2,1,0:T(8,128)} %mat_ref.1) | copy-start | bytes 98308
  3.3 0.7 %copy-start.4 = (f32[8]{0:T(128)S(1)}, f32[8]{0:T(128)}, u32[]{:S(2)}) copy-start(f32[8]{0:T(128)} %perm_tab.1) | copy-start | bytes 100
  3.9 0.7 %copy-start.5 = (f32[8]{0:T(128)S(1)}, f32[8]{0:T(128)}, u32[]{:S(2)}) copy-start(f32[8]{0:T(128)} %poro_tab.1) | copy-start | bytes 100
where the time goes:
time: 57.4 us; the launch traced here: 57.1 us
  Pallas kernels  51.9 us (90%)
  local copies, waits for them, and re-layouts  5.19 us (9%)
    pallas_call x1, Pallas kernels, local(): pl.pallas_call(functools.partial(kernel, n_grp, n_sub), out_shape=jax.Sha...  51.9 us
    unnamed x13, local copies, waits for them, and re-layouts  5.19 us

commit v1 on v0

v1 whole, which is shorter than its diff:
```python
import functools

import jax
import jax.numpy as jnp
from jax import lax
from jax.experimental import pallas as pl
from jax.experimental.pallas import tpu as pltpu
from jax.sharding import PartitionSpec as P

CX = 8
AGG = 4
ITERS = 4
DISP = 0.2
CPL_P = 0.5
CPL_S = 0.3
OMEGA = 0.7
OMEGA_C = 0.7
THETA = 0.5

PITCH = 12
BASE = 8
ROWS = 160
LANES = 128
MESH = pl.DeviceIdType.MESH

SIDES = [(-1, 0), (1, 0), (0, -1), (0, 1), (-1, -1), (-1, 1), (1, -1), (1, 1)]
FAR = [(-1, -2), (-1, 2), (1, -2), (1, 2), (0, -2), (0, 2)]
PARTNERS = FAR + SIDES[4:] + SIDES[:4]
NEAR = [(0, -2), (0, 2), (0, -1), (0, 1)]

MAT, HEAD, F0, F1, F2, COT = 0, 1, 2, 3, 4, 5
TX, TXM, TY, TYM, TZ, TZM, SX, SXM, SY, SYM, SZ, SZM, BPP, BPC, BCP, BCC, IPP, IPC, ICP, ICC = range(20)
N_COEF = 20
N_CBLK = 13
C_ROWS = 64
ROUNDS = ITERS - 1


def row(x, y):
    return BASE + (x + 2) * PITCH + y + 2


def rows(x, y, count=8):
    return pl.ds(row(x, y), count)


def column(y):
    return pl.ds(row(0, y), 8, stride=PITCH)


def setup_slots(low, along):
    if low:
        pairs = [(MAT, -2), (MAT, -1), (HEAD, -2), (HEAD, -1), (along, -2)]
        one = -1
    else:
        pairs = [(MAT, 8), (MAT, 9), (HEAD, 8), (HEAD, 9)]
        one = 8
    return pairs + [(field, one) for field in (F0, F1, F2, COT, COT + 1)]


def field_slots(low):
    return [(f, layer) for f in (0, 1) for layer in ((-2, -1) if low else (8, 9))]


def slots_of(side, setup):
    dx, dy = side
    if dx != 0:
        return setup_slots(dx < 0, F0) if setup else field_slots(dx < 0)
    return setup_slots(dy < 0, F1) if setup else field_slots(dy < 0)


def pack(side, setup, src, dst, lead):
    dx, dy = side
    for slot, (field, layer) in enumerate(slots_of(side, setup)):
        if dy == 0:
            dst[lead + (pl.ds(8 * slot, 8),)] = src[field, rows(layer % 8, 0), :]
        elif dx == 0:
            dst[lead + (pl.ds(8 * slot, 8),)] = src[field, column(layer % 8), :]
        else:
            dst[lead + (pl.ds(2 * slot, 2),)] = src[field, rows(layer % 8, 6 if dy < 0 else 0, 2), :]


def unpack(side, setup, src, lead, dst, valid):
    dx, dy = side

    def seen(field, value):
        return jnp.where(valid, value, -1.0) if setup and field == MAT else value

    for slot, (field, layer) in enumerate(slots_of(side, setup)):
        if dy == 0:
            dst[field, rows(layer, 0), :] = seen(field, src[lead + (pl.ds(8 * slot, 8),)])
        elif dx == 0:
            dst[field, column(layer), :] = seen(field, src[lead + (pl.ds(8 * slot, 8),)])
        else:
            dst[field, rows(layer, -2 if dy < 0 else 8, 2), :] = seen(field, src[lead + (pl.ds(2 * slot, 2),)])


def next_lane(value, by=1):
    return pltpu.roll(value, LANES - by, 1)


def last_lane(value, by=1):
    return pltpu.roll(value, by, 1)


def lane_sum(value):
    lane = lax.broadcasted_iota(jnp.int32, value.shape, 1)
    total = value + next_lane(value)
    total = total + next_lane(total, 2)
    total = jnp.where(lane % AGG == 0, total, 0.0)
    total = total + last_lane(total)
    return total + last_lane(total, 2)


def four_sum(value):
    total = value + pltpu.roll(value, 7, 0)
    return total + pltpu.roll(total, 6, 0)


def couple(co, field, lo, n):
    here = pl.ds(lo, n)
    out = []
    for f, first in ((0, TX), (1, SX)):
        mid = field[f, here, :]
        total = co[first, here, :] * field[f, pl.ds(lo + PITCH, n), :]
        total = total + co[first + 1, here, :] * field[f, pl.ds(lo - PITCH, n), :]
        total = total + co[first + 2, here, :] * field[f, pl.ds(lo + 1, n), :]
        total = total + co[first + 3, here, :] * field[f, pl.ds(lo - 1, n), :]
        total = total + co[first + 4, here, :] * next_lane(mid)
        total = total + co[first + 5, here, :] * last_lane(mid)
        out += [mid, total]
    return out


def kernel(
    n_grp,
    n_sub,
    cot_hbm,
    head_hbm,
    mat_hbm,
    flag_hbm,
    perm_hbm,
    poro_hbm,
    out_ref,
    cot_ref,
    head_ref,
    mat_ref,
    flag_ref,
    perm_tab,
    poro_tab,
    ext,
    perm,
    poro,
    mask,
    face,
    co,
    adj,
    inc,
    res,
    grd,
    mid,
    fin,
    ssend,
    srecv,
    rsend,
    rrecv,
    ksend,
    krecv,
    cagg,
    ring,
    cco,
    cres,
    layer,
    l_sem,
    s_send,
    s_recv,
    r_send,
    r_recv,
    k_send,
    k_recv,
):
    g = lax.axis_index("grp")
    s = lax.axis_index("sub")

    def device(dx, dy):
        return {"grp": lax.rem(g + dx + n_grp, n_grp), "sub": lax.rem(s + dy + n_sub, n_sub)}

    def fits(dx, dy):
        found = []
        for at, count, step in ((g, n_grp, dx), (s, n_sub, dy)):
            if step < 0:
                found.append(at >= -step)
            elif step > 0:
                found.append(at < count - step)
        return found[0] if len(found) == 1 else jnp.logical_and(*found)

    loads = [
        pltpu.make_async_copy(src, dst, l_sem.at[i])
        for i, (src, dst) in enumerate((
            (mat_hbm, mat_ref), (head_hbm, head_ref), (flag_hbm, flag_ref), (cot_hbm, cot_ref), (perm_hbm, perm_tab), (poro_hbm, poro_tab)
        ))
    ]
    for load in loads:
        load.start()

    barrier = pltpu.get_barrier_semaphore()
    expected = jnp.int32(0)
    for dx, dy in PARTNERS:
        there = fits(dx, dy)

        @pl.when(there)
        def _():
            pl.semaphore_signal(barrier, inc=1, device_id=device(dx, dy), device_id_type=MESH)

        expected = expected + there.astype(jnp.int32)

    def rows_of(side, setup):
        dx, dy = side
        if side in FAR:
            return 0
        if setup:
            count = len(slots_of(side, True)) * (2 if dx != 0 and dy != 0 else 8)
            return -(-count // 8) * 8
        return 8 if dx != 0 and dy != 0 else 32

    def setup_copy(i):
        dx, dy = SIDES[i]
        part = pl.ds(0, rows_of((dx, dy), True))
        return pltpu.make_async_remote_copy(
            ssend.at[i, part], srecv.at[i, part], s_send.at[i], s_recv.at[i], device_id=device(-dx, -dy), device_id_type=MESH
        )

    def round_copy(i, k):
        dx, dy = PARTNERS[i]
        part = pl.ds(0, rows_of((dx, dy), False) + (16 if dx == 0 else 8))
        return pltpu.make_async_remote_copy(
            rsend.at[k, i, part], rrecv.at[k, i, part], r_send.at[k, i], r_recv.at[k, i], device_id=device(-dx, -dy), device_id_type=MESH
        )

    def coef_copy(j):
        dx, dy = NEAR[j]
        return pltpu.make_async_remote_copy(
            ksend, krecv.at[j], k_send.at[j], k_recv.at[j], device_id=device(-dx, -dy), device_id_type=MESH
        )

    def when_sent(side, act):
        pl.when(fits(-side[0], -side[1]))(act)

    def when_there(side, act):
        pl.when(fits(*side))(act)

    zero_rows = jnp.zeros((ROWS, LANES), jnp.float32)
    ext[MAT] = zero_rows - 1.0
    for f in range(1, 7):
        ext[f] = zero_rows
    mask[...] = zero_rows
    perm[...] = zero_rows
    poro[...] = zero_rows
    for f in range(2):
        adj[f] = zero_rows
        inc[f] = zero_rows
        grd[f] = zero_rows
        mid[f] = zero_rows
    for m in range(9):
        face[m, pl.ds(0, 32), :] = jnp.zeros((32, LANES), jnp.float32)
    for x in range(-1, 9):
        mask[rows(x, -1, 10), :] = jnp.ones((10, LANES), jnp.float32)
    for i, side in enumerate(SIDES):

        @pl.when(jnp.logical_not(fits(*side)))
        def _():
            srecv[i] = jnp.zeros((80, LANES), jnp.float32)

    for i, side in enumerate(PARTNERS):

        @pl.when(jnp.logical_not(fits(*side)))
        def _():
            for k in range(ROUNDS):
                rrecv[k, i] = jnp.zeros((48, LANES), jnp.float32)

    for j, side in enumerate(NEAR):

        @pl.when(jnp.logical_not(fits(*side)))
        def _():
            krecv[j] = jnp.zeros((C_ROWS, LANES), jnp.float32)

    for load in loads:
        load.wait()
    for x in range(8):
        ext[MAT, rows(x, 0), :] = mat_ref[x].astype(jnp.float32)
        ext[HEAD, rows(x, 0), :] = head_ref[x]
        for d in range(3):
            ext[F0 + d, rows(x, 0), :] = flag_ref[d, x].astype(jnp.float32)
        for f in range(2):
            ext[COT + f, rows(x, 0), :] = cot_ref[f, x]
    for i, side in enumerate(SIDES):
        pack(side, True, ext, ssend, (i,))

    pl.semaphore_wait(barrier, expected)
    for i in reversed(range(8)):
        when_sent(SIDES[i], lambda: setup_copy(i).start())

    def look_up(mats):
        perm_here = jnp.zeros_like(mats)
        poro_here = jnp.zeros_like(mats)
        for level in range(perm_tab.shape[0]):
            same = mats == float(level)
            perm_here = jnp.where(same, perm_tab[level], perm_here)
            poro_here = jnp.where(same, poro_tab[level], poro_here)
        return perm_here, poro_here

    def one_face(perm_here, head_here, perm_next, head_next, upwind):
        both = perm_here + perm_next
        trans = 2.0 * perm_here * perm_next / jnp.where(both > 0.0, both, 1.0)
        flux = trans * (0.5 + jnp.abs(head_here - head_next))
        return trans, upwind * flux, (1.0 - upwind) * flux

    def look_up_rows(first, end, n):
        for lo in range(first, end, n):
            here = pl.ds(lo, n)
            perm[here, :], poro[here, :] = look_up(ext[MAT, here, :])

    def face_rows(first, end, n):
        for lo in range(first, end, n):
            here = pl.ds(lo, n)
            perm_here, head_here = perm[here, :], ext[HEAD, here, :]
            lane = lax.broadcasted_iota(jnp.int32, (n, LANES), 1)
            for d in range(3):
                if d < 2:
                    there = pl.ds(lo + (PITCH, 1)[d], n)
                    perm_next, head_next = perm[there, :], ext[HEAD, there, :]
                else:
                    perm_next = jnp.where(lane == LANES - 1, 0.0, next_lane(perm_here))
                    head_next = next_lane(head_here)
                values = one_face(perm_here, head_here, perm_next, head_next, ext[F0 + d, here, :])
                for m in range(3):
                    face[3 * d + m, here, :] = values[m]

    look_up_rows(32, 128, 32)
    face_rows(32, 128, 24)

    def put(block, cx, cy, value):
        cagg[pl.ds(4 * block + 2 * cx + cy, 1), :] = value

    def put_y(block, cx, value):
        value = four_sum(value)
        put(block, cx, 0, value[0:1])
        put(block, cx, 1, value[4:5])

    def put_x(block, cy, value):
        value = four_sum(value)
        put(block, 0, cy, value[0:1])
        put(block, 1, cy, value[4:5])

    cagg[...] = jnp.zeros((64, LANES), jnp.float32)
    lane = lax.broadcasted_iota(jnp.int32, (8, LANES), 1)
    for cx in range(2):
        sums = [0.0] * 5
        for x in range(4 * cx, 4 * cx + 4):
            here = rows(x, 0)
            zs = [face[6 + m, here, :] for m in range(3)]
            out = face[1, here, :] + face[4, here, :] + zs[1]
            out = out + face[2, rows(x - 1, 0), :] + face[5, rows(x, -1), :] + last_lane(zs[2])
            sums = [old + new for old, new in zip(sums, [poro[here, :], out] + zs)]
        for m in range(2, 5):
            sums[m] = jnp.where(lane % AGG == AGG - 1, sums[m], 0.0)
        for b, value in zip((0, 1, 12, 13, 14), sums):
            put_y(b, cx, value)
    for b, cx, m in ((2, 0, 0), (3, 1, 0), (4, 0, 1), (5, 0, 2), (6, 1, 2)):
        put_y(b, cx, face[m, rows(3, 0), :])
    for b, cy, m in ((7, 0, 0), (8, 1, 0), (9, 0, 1), (10, 0, 2), (11, 1, 2)):
        put_x(b, cy, face[3 + m, column(3), :])
    for f in range(2):
        for cx in range(2):
            total = ext[COT + f, rows(4 * cx, 0), :]
            for x in range(4 * cx + 1, 4 * cx + 4):
                total = total + ext[COT + f, rows(x, 0), :]
            total = four_sum(total)
            first = 4 * f + 2 * cx
            ring[pl.ds(first, 1), :] = total[0:1]
            ring[pl.ds(first + 1, 1), :] = total[4:5]
    ksend[pl.ds(52, 8), :] = lane_sum(ring[pl.ds(0, 8), :])
    ksend[pl.ds(60, 4), :] = jnp.zeros((4, LANES), jnp.float32)

    def take(i):
        when_there(SIDES[i], lambda: setup_copy(i).wait_recv())
        unpack(SIDES[i], True, srecv, (i,), ext, fits(*SIDES[i]))

    for i in range(4):
        take(i)

    def edge(axis, here, there):
        perm_here, _ = look_up(ext[MAT, here, :])
        perm_next, _ = look_up(ext[MAT, there, :])
        return one_face(perm_here, ext[HEAD, here, :], perm_next, ext[HEAD, there, :], ext[F0 + axis, here, :])

    trans, _, lower = edge(0, rows(-1, 0), rows(0, 0))
    put_y(3, 0, trans)
    put_y(6, 0, lower)
    trans, upper, _ = edge(0, rows(7, 0), rows(8, 0))
    put_y(2, 1, trans)
    put_y(4, 1, upper)
    trans, _, lower = edge(1, column(-1), column(0))
    put_x(8, 0, trans)
    put_x(11, 0, lower)
    trans, upper, lower = edge(1, column(7), column(8))
    put_x(7, 1, trans)
    put_x(9, 1, upper)
    put_x(10, 1, lower)
    cagg[...] = lane_sum(cagg[...])

    def block(b):
        return cagg[pl.ds(4 * b, 4), :]

    place = lax.broadcasted_iota(jnp.int32, (4, LANES), 0)
    store = block(0)
    t_z, a_z, b_z = block(12), block(13), block(14)
    edge_sum = block(2) + block(3) + block(7) + block(8) + t_z + last_lane(t_z, AGG)
    edge_out = block(4) + block(6) + block(9) + block(11) + a_z + last_lane(b_z, AGG)
    out = block(1) + jnp.where(place < 2, block(6), block(4)) + jnp.where(place % 2 == 0, block(11), block(9))
    cpp, cpc, ccp, ccc = store + edge_sum, -CPL_S * out, CPL_P * store, store + DISP * edge_sum + edge_out
    scale = OMEGA_C / (cpp * ccc - cpc * ccp)
    t_x, t_y = block(2), block(7)
    for b, value in enumerate((
        ccc * scale, -cpc * scale, -ccp * scale, cpp * scale,
        t_y, DISP * t_y + block(9), DISP * t_y + block(10),
        t_z, DISP * t_z + a_z, DISP * t_z + b_z,
        t_x, DISP * t_x + block(4), DISP * t_x + block(5),
    )):
        ksend[pl.ds(4 * b, 4), :] = value
    for j in range(4):
        when_sent(NEAR[j], lambda: coef_copy(j).start())

    for i in range(4, 8):
        take(i)
    look_up_rows(0, ROWS, 32)
    face_rows(0, 144, 24)
    for lo in range(16, 144, 16):
        here = pl.ds(lo, 16)
        total = jnp.zeros((16, LANES), jnp.float32)
        out = total
        for d in range(3):
            trans, upper, lower = (face[3 * d + m, here, :] for m in range(3))
            if d < 2:
                back = pl.ds(lo - (PITCH, 1)[d], 16)
                trans_m, lower_m = face[3 * d, back, :], face[3 * d + 2, back, :]
            else:
                trans_m, lower_m = last_lane(trans), last_lane(lower)
            co[TX + 2 * d, here, :] = trans
            co[TX + 2 * d + 1, here, :] = trans_m
            co[SX + 2 * d, here, :] = DISP * trans + upper
            co[SX + 2 * d + 1, here, :] = DISP * trans_m + lower_m
            total = total + trans + trans_m
            out = out + upper + lower_m
        store = poro[here, :]
        bpp, bpc, bcp, bcc = store + total, -CPL_S * out, CPL_P * store, store + DISP * total + out
        inside = jnp.logical_and(store > 0.0, mask[here, :] > 0.0)
        determ = jnp.where(inside, bpp * bcc - bpc * bcp, 1.0)
        scale = jnp.where(inside, OMEGA / determ, 0.0)
        for at, value in (
            (BPP, bpp), (BPC, bpc), (BCP, bcp), (BCC, bcc),
            (IPP, bcc * scale), (IPC, -bpc * scale), (ICP, -bcp * scale), (ICC, bpp * scale),
        ):
            co[at, here, :] = value

    def fine_solve(src, at):
        for lo in range(16, 144, 32):
            here = pl.ds(lo, 32)
            r_p, r_c = src[at, here, :], src[at + 1, here, :]
            grd[0, here, :] = co[IPP, here, :] * r_p + co[IPC, here, :] * r_c
            grd[1, here, :] = co[ICP, here, :] * r_p + co[ICC, here, :] * r_c
        for lo in range(16, 144, 16):
            here = pl.ds(lo, 16)
            z_p, s_p, z_c, s_c = couple(co, grd, lo, 16)
            mid[0, here, :] = (2.0 - OMEGA) * z_p + co[IPP, here, :] * s_p + co[IPC, here, :] * s_c
            mid[1, here, :] = (2.0 - OMEGA) * z_c + co[ICP, here, :] * s_p + co[ICC, here, :] * s_c
        for lo in range(32, 128, 16):
            here = pl.ds(lo, 16)
            z_p, s_p, z_c, s_c = couple(co, mid, lo, 16)
            fin[0, here, :] = (1.0 - OMEGA) * z_p + grd[0, here, :] + co[IPP, here, :] * s_p + co[IPC, here, :] * s_c
            fin[1, here, :] = (1.0 - OMEGA) * z_c + grd[1, here, :] + co[ICP, here, :] * s_p + co[ICC, here, :] * s_c

    def coarse_solve():
        ipp, ipc, icp, icc = ([cco[b, cx] for cx in range(2)] for b in range(4))
        t_y, a_y, b_y, t_z, a_z, b_z = ([cco[b, cx] for cx in range(2)] for b in range(4, 10))
        t_x, a_x, b_x = (cco[b, 0] for b in range(10, 13))
        ahead = {0: (t_y, t_z), 1: (a_y, a_z)}
        behind = {
            0: ([pltpu.roll(v, 1, 0) for v in t_y], [last_lane(v, AGG) for v in t_z]),
            1: ([pltpu.roll(v, 1, 0) for v in b_y], [last_lane(v, AGG) for v in b_z]),
        }
        across = {0: (t_x, t_x), 1: (a_x, b_x)}
        r = [[cres[2 * f + cx] for cx in range(2)] for f in range(2)]
        base = [
            [ipp[cx] * r[0][cx] + ipc[cx] * r[1][cx] for cx in range(2)],
            [icp[cx] * r[0][cx] + icc[cx] * r[1][cx] for cx in range(2)],
        ]
        z = base
        for sweep in range(3):
            acc = [[None] * 2 for f in range(2)]
            for f in range(2):
                for cx in range(2):
                    v = z[f][cx]
                    total = across[f][cx] * z[f][1 - cx]
                    total = total + ahead[f][0][cx] * pltpu.roll(v, 7, 0)
                    total = total + behind[f][0][cx] * pltpu.roll(v, 1, 0)
                    total = total + ahead[f][1][cx] * next_lane(v, AGG)
                    acc[f][cx] = total + behind[f][1][cx] * last_lane(v, AGG)
            z = [
                [(1.0 - OMEGA_C) * z[0][cx] + base[0][cx] + ipp[cx] * acc[0][cx] + ipc[cx] * acc[1][cx] for cx in range(2)],
                [(1.0 - OMEGA_C) * z[1][cx] + base[1][cx] + icp[cx] * acc[0][cx] + icc[cx] * acc[1][cx] for cx in range(2)],
            ]
        upper = lax.broadcasted_iota(jnp.int32, (8, LANES), 0) < AGG
        return [
            [
                jnp.where(upper, jnp.broadcast_to(v[3:4], (8, LANES)), jnp.broadcast_to(v[4:5], (8, LANES)))
                for v in z[f]
            ]
            for f in range(2)
        ]

    def update():
        grown = coarse_solve()
        for f in range(2):
            for x in range(8):
                here = rows(x, 0)
                more = THETA * (fin[f, here, :] + grown[f][x // 4])
                new = adj[f, here, :] + more
                inc[f, here, :] = more
                adj[f, here, :] = new
                out_ref[f, x] = new

    def send(k):
        for lo in range(16, 144, 16):
            here = pl.ds(lo, 16)
            z_p, s_p, z_c, s_c = couple(co, inc, lo, 16)
            res[0, here, :] = co[BPP, here, :] * z_p + co[BPC, here, :] * z_c - s_p
            res[1, here, :] = co[BCP, here, :] * z_p + co[BCC, here, :] * z_c - s_c

        def place(at, value):
            ring[pl.ds(at, 1), :] = value

        for f in range(2):
            for cx in range(2):
                total = res[f, rows(4 * cx, 0), :]
                for x in range(4 * cx + 1, 4 * cx + 4):
                    total = total + res[f, rows(x, 0), :]
                total = four_sum(total)
                place(8 * f + 4 * cx + 1, total[0:1])
                place(8 * f + 4 * cx + 2, total[4:5])
            for at, y in ((0, -1), (3, 8)):
                total = four_sum(res[f, column(y), :])
                place(8 * f + at, total[0:1])
                place(8 * f + 4 + at, total[4:5])
            for at, x in ((16, -1), (20, 8)):
                total = four_sum(res[f, rows(x, 0), :])
                place(at + 2 * f, total[0:1])
                place(at + 2 * f + 1, total[4:5])
        ring[...] = lane_sum(ring[...])
        along, beside = ring[pl.ds(0, 16), :], ring[pl.ds(16, 8), :]
        for i, side in enumerate(PARTNERS):
            if side not in FAR:
                pack(side, False, adj, rsend, (k, i))
            at = rows_of(side, False)
            if side[0] == 0:
                rsend[k, i, pl.ds(at, 16), :] = along
            else:
                rsend[k, i, pl.ds(at, 8), :] = beside
            when_sent(side, lambda: round_copy(i, k).start())

    def receive(k):
        for i, side in enumerate(PARTNERS):
            when_there(side, lambda: round_copy(i, k).wait_recv())
            if side not in FAR:
                unpack(side, False, rrecv, (k, i), adj, None)
        for f in range(2):
            for cx in range(2):
                item = 2 * f + cx

                def along(dy, first, count):
                    i = PARTNERS.index((0, dy))
                    return rrecv[k, i, pl.ds(rows_of((0, dy), False) + 4 * item + first, count), :]

                layer[0, item, pl.ds(0, 4), :] = along(-1, 0, 4)
                layer[0, item, pl.ds(4, 4), :] = along(1, 0, 4)
                layer[1, item, pl.ds(0, 2), :] = along(-2, 2, 2)
                layer[1, item, pl.ds(2, 4), :] = ring[pl.ds(4 * item, 4), :]
                layer[1, item, pl.ds(6, 2), :] = along(2, 0, 2)
                dx = 2 * cx - 1
                for dy in range(-2, 3):
                    first, count = max(2 * dy + 3, 0), 1 if abs(dy) == 2 else 2
                    at = rows_of((dx, dy), False) + (4 if dx < 0 else 0) + 2 * f + (1 if dy == -2 else 0)
                    layer[2, item, pl.ds(first, count), :] = rrecv[k, PARTNERS.index((dx, dy)), pl.ds(at, count), :]
                cres[item] = cres[item] - layer[0, item] - layer[1, item] - layer[2, item]
        for lo in range(16, 144, 16):
            here = pl.ds(lo, 16)
            z_p, s_p, z_c, s_c = couple(co, adj, lo, 16)
            res[0, here, :] = ext[COT, here, :] + s_p - co[BPP, here, :] * z_p - co[BPC, here, :] * z_c
            res[1, here, :] = ext[COT + 1, here, :] + s_c - co[BCP, here, :] * z_p - co[BCC, here, :] * z_c

    fine_solve(ext, COT)

    for j in range(4):
        when_there(NEAR[j], lambda: coef_copy(j).wait_recv())
    for item in range(2 * N_CBLK + 4):

        def put_coarse(where, value):
            if item < 2 * N_CBLK:
                cco[item // 2, item % 2, where, :] = value
            else:
                cres[item - 2 * N_CBLK, where, :] = value

        put_coarse(pl.ds(0, 1), krecv[0, pl.ds(2 * item + 1, 1), :])
        put_coarse(pl.ds(1, 2), krecv[2, pl.ds(2 * item, 2), :])
        put_coarse(pl.ds(3, 2), ksend[pl.ds(2 * item, 2), :])
        put_coarse(pl.ds(5, 2), krecv[3, pl.ds(2 * item, 2), :])
        put_coarse(pl.ds(7, 1), krecv[1, pl.ds(2 * item, 1), :])
    update()
    send(0)

    def step(k, carry):
        receive(k - 1)
        fine_solve(res, 0)
        update()
        pl.when(k < ITERS - 1)(lambda: send(k))
        return carry

    lax.fori_loop(1, ITERS, step, 0)

    for i, side in enumerate(SIDES):
        when_sent(side, lambda: setup_copy(i).wait_send())
    for i, side in enumerate(PARTNERS):

        def sent():
            for k in range(ROUNDS):
                round_copy(i, k).wait_send()

        when_sent(side, sent)
    for j, side in enumerate(NEAR):
        when_sent(side, lambda: coef_copy(j).wait_send())


def solution(mesh):
    n_grp, n_sub = mesh.shape["grp"], mesh.shape["sub"]

    def local(cotangent, head, materials, flags, perm_table, poro_table):
        def tile(*shape):
            return pltpu.VMEM(shape + (LANES,), jnp.float32)

        dma = pltpu.SemaphoreType.DMA
        vmem = pl.BlockSpec(memory_space=pltpu.VMEM)
        hbm = pl.BlockSpec(memory_space=pltpu.HBM)
        n_part = len(PARTNERS)
        return pl.pallas_call(
            functools.partial(kernel, n_grp, n_sub),
            out_shape=jax.ShapeDtypeStruct(cotangent.shape, jnp.float32),
            in_specs=[hbm] * 6,
            out_specs=vmem,
            scratch_shapes=[
                pltpu.VMEM(cotangent.shape, jnp.float32),
                pltpu.VMEM(head.shape, jnp.float32),
                pltpu.VMEM(materials.shape, jnp.int32),
                pltpu.VMEM(flags.shape, jnp.int32),
                pltpu.SMEM(perm_table.shape, jnp.float32),
                pltpu.SMEM(poro_table.shape, jnp.float32),
                tile(7, ROWS),
                tile(ROWS),
                tile(ROWS),
                tile(ROWS),
                tile(9, ROWS),
                tile(N_COEF, ROWS),
                tile(2, ROWS),
                tile(2, ROWS),
                tile(2, ROWS),
                tile(2, ROWS),
                tile(2, ROWS),
                tile(2, ROWS),
                tile(8, 80),
                tile(8, 80),
                tile(ROUNDS, n_part, 48),
                tile(ROUNDS, n_part, 48),
                tile(C_ROWS),
                tile(4, C_ROWS),
                tile(64),
                tile(24),
                tile(N_CBLK, 2, 8),
                tile(4, 8),
                tile(3, 4, 8),
                dma((6,)),
                dma((8,)),
                dma((8,)),
                dma((ROUNDS, n_part)),
                dma((ROUNDS, n_part)),
                dma((4,)),
                dma((4,)),
            ],
            compiler_params=pltpu.CompilerParams(
                collective_id=0, has_side_effects=True, vmem_limit_bytes=32 * 1024 * 1024
            ),
        )(cotangent, head, materials, flags, perm_table, poro_table)

    return jax.shard_map(
        local,
        mesh=mesh,
        in_specs=(
            P(None, "grp", "sub", None),
            P("grp", "sub", None),
            P("grp", "sub", None),
            P(None, "grp", "sub", None),
            P(),
            P(),
        ),
        out_specs=P(None, "grp", "sub", None),
        check_vma=False,
    )
```

time: 57.4 us -> 37.5 us (0.65)
  the two profiles are of different devices: /device:TPU:1 before, /device:TPU:6 now
where the time goes in v1:
time: 37.5 us; the launch traced here: 37.2 us
  Pallas kernels  32 us (85%)
  local copies, waits for them, and re-layouts  5.19 us (14%)
    pallas_call x1, Pallas kernels, local(): pl.pallas_call(functools.partial(kernel, n_grp, n_sub), out_shape=jax.Sha...  32 us
    unnamed x13, local copies, waits for them, and re-layouts  5.19 us

profile of v1, /device:TPU:6, one launch (start us, length us, event | category | flops | bytes accessed | tf_op | source)
XLA Modules:
  0.0 37.2 jit_solution(10885909931559920723)
XLA Ops:
  0.0 0.0 copy-start
  0.0 0.9 %copy-done = s32[3,8,8,128]{3,2,1,0:T(8,128)S(1)} copy-done((s32[3,8,8,128]{3,2,1,0:T(8,128)S(1)}, s32[3,8,8,128]{3,2,1,0:T(8,128)}, u32[]{:S(2)}) %copy-start) | copy-done | bytes 98328
  0.9 0.0 copy-start.1
  0.9 0.8 %copy-done.1 = f32[2,8,8,128]{3,2,1,0:T(8,128)S(1)} copy-done((f32[2,8,8,128]{3,2,1,0:T(8,128)S(1)}, f32[2,8,8,128]{3,2,1,0:T(8,128)}, u32[]{:S(2)}) %copy-start.1) | copy-done | bytes 65560
  1.7 0.0 copy-start.2
  1.7 0.8 %copy-done.2 = f32[8,8,128]{2,1,0:T(8,128)S(1)} copy-done((f32[8,8,128]{2,1,0:T(8,128)S(1)}, f32[8,8,128]{2,1,0:T(8,128)}, u32[]{:S(2)}) %copy-start.2) | copy-done | bytes 32792
  2.5 0.0 copy-start.3
  2.5 0.8 %copy-done.3 = s32[8,8,128]{2,1,0:T(8,128)S(1)} copy-done((s32[8,8,128]{2,1,0:T(8,128)S(1)}, s32[8,8,128]{2,1,0:T(8,128)}, u32[]{:S(2)}) %copy-start.3) | copy-done | bytes 32792
  3.3 0.0 copy-start.4
  3.3 0.7 %copy-done.4 = f32[8]{0:T(128)S(1)} copy-done((f32[8]{0:T(128)S(1)}, f32[8]{0:T(128)}, u32[]{:S(2)}) %copy-start.4) | copy-done | bytes 56
  3.9 0.0 copy-start.5
  3.9 0.7 %copy-done.5 = f32[8]{0:T(128)S(1)} copy-done((f32[8]{0:T(128)S(1)}, f32[8]{0:T(128)}, u32[]{:S(2)}) %copy-start.5) | copy-done | bytes 56
  4.6 32.0 %shard_map.64 = f32[2,8,8,128]{3,2,1,0:T(8,128)S(1)} custom-call(f32[2,8,8,128]{3,2,1,0:T(8,128)S(1)} %copy-done.1, f32[8,8,128]{2,1,0:T(8,128)S(1)} %copy-done.2, s32[8,8,128]{2,1,0:T(8,128)S(1)} %copy-done.3, s32[3,8,8,128]{3,2,1,0:T(8,128)S(1)} %copy-done, f32[8]{0:T(128)S(1)} %copy-done.4, f32[8]{0:T(128)S(1)} %copy-done.5), custom_call_target="tpu_custom_call" | custom-call | tf_op jit(solution)/shard_map/pallas_call | solution.py:654
  36.6 0.6 %copy.8 = f32[2,8,8,128]{3,2,1,0:T(8,128)} copy(f32[2,8,8,128]{3,2,1,0:T(8,128)S(1)} %shard_map.64) | data formatting | bytes 131072
Async XLA Ops:
  0.0 0.9 %copy-start = (s32[3,8,8,128]{3,2,1,0:T(8,128)S(1)}, s32[3,8,8,128]{3,2,1,0:T(8,128)}, u32[]{:S(2)}) copy-start(s32[3,8,8,128]{3,2,1,0:T(8,128)} %flag_hbm.1) | copy-start | bytes 294916
  0.9 0.8 %copy-start.1 = (f32[2,8,8,128]{3,2,1,0:T(8,128)S(1)}, f32[2,8,8,128]{3,2,1,0:T(8,128)}, u32[]{:S(2)}) copy-start(f32[2,8,8,128]{3,2,1,0:T(8,128)} %cot_hbm.1) | copy-start | bytes 196612
  1.7 0.8 %copy-start.2 = (f32[8,8,128]{2,1,0:T(8,128)S(1)}, f32[8,8,128]{2,1,0:T(8,128)}, u32[]{:S(2)}) copy-start(f32[8,8,128]{2,1,0:T(8,128)} %head_hbm.1) | copy-start | bytes 98308
  2.5 0.8 %copy-start.3 = (s32[8,8,128]{2,1,0:T(8,128)S(1)}, s32[8,8,128]{2,1,0:T(8,128)}, u32[]{:S(2)}) copy-start(s32[8,8,128]{2,1,0:T(8,128)} %mat_hbm.1) | copy-start | bytes 98308
  3.3 0.7 %copy-start.4 = (f32[8]{0:T(128)S(1)}, f32[8]{0:T(128)}, u32[]{:S(2)}) copy-start(f32[8]{0:T(128)} %perm_hbm.1) | copy-start | bytes 100
  3.9 0.7 %copy-start.5 = (f32[8]{0:T(128)S(1)}, f32[8]{0:T(128)}, u32[]{:S(2)}) copy-start(f32[8]{0:T(128)} %poro_hbm.1) | copy-start | bytes 100

commit v2 on v1

--- a/solution.py
+++ b/solution.py
@@ -49,13 +49,10 @@
 
 
 def setup_slots(low, along):
-    if low:
-        pairs = [(MAT, -2), (MAT, -1), (HEAD, -2), (HEAD, -1), (along, -2)]
-        one = -1
-    else:
-        pairs = [(MAT, 8), (MAT, 9), (HEAD, 8), (HEAD, 9)]
-        one = 8
-    return pairs + [(field, one) for field in (F0, F1, F2, COT, COT + 1)]
+    one, two = (-1, -2) if low else (8, 9)
+    first = [(MAT, one), (HEAD, one), (along, one)]
+    others = [(field, one) for field in (F0, F1, F2) if field != along]
+    return first + others + [(MAT, two), (HEAD, two)] + ([(along, two)] if low else []) + [(COT, one), (COT + 1, one)]
 
 
 def field_slots(low):
@@ -80,13 +77,13 @@
             dst[lead + (pl.ds(2 * slot, 2),)] = src[field, rows(layer % 8, 6 if dy < 0 else 0, 2), :]
 
 
-def unpack(side, setup, src, lead, dst, valid):
+def unpack(side, setup, src, lead, dst, valid, first=0, end=None):
     dx, dy = side
 
     def seen(field, value):
         return jnp.where(valid, value, -1.0) if setup and field == MAT else value
 
-    for slot, (field, layer) in enumerate(slots_of(side, setup)):
+    for slot, (field, layer) in list(enumerate(slots_of(side, setup)))[first:end]:
         if dy == 0:
             dst[field, rows(layer, 0), :] = seen(field, src[lead + (pl.ds(8 * slot, 8),)])
         elif dx == 0:
@@ -183,7 +180,7 @@
     s = lax.axis_index("sub")
 
     def device(dx, dy):
-        return {"grp": lax.rem(g + dx + n_grp, n_grp), "sub": lax.rem(s + dy + n_sub, n_sub)}
+        return {"grp": g + dx, "sub": s + dy}
 
     def fits(dx, dy):
         found = []
@@ -205,7 +202,7 @@
 
     barrier = pltpu.get_barrier_semaphore()
     expected = jnp.int32(0)
-    for dx, dy in PARTNERS:
+    for dx, dy in SIDES:
         there = fits(dx, dy)
 
         @pl.when(there)
@@ -223,11 +220,16 @@
             return -(-count // 8) * 8
         return 8 if dx != 0 and dy != 0 else 32
 
-    def setup_copy(i):
+    def setup_copy(i, first=False):
         dx, dy = SIDES[i]
-        part = pl.ds(0, rows_of((dx, dy), True))
+        start, end, at = 0, rows_of((dx, dy), True), i
+        if first:
+            end, at = 24, 8 + i
+        elif i < 4:
+            start = 24
+        part = pl.ds(start, end - start)
         return pltpu.make_async_remote_copy(
-            ssend.at[i, part], srecv.at[i, part], s_send.at[i], s_recv.at[i], device_id=device(-dx, -dy), device_id_type=MESH
+            ssend.at[i, part], srecv.at[i, part], s_send.at[at], s_recv.at[at], device_id=device(-dx, -dy), device_id_type=MESH
         )
 
     def round_copy(i, k):
@@ -297,6 +299,8 @@
         pack(side, True, ext, ssend, (i,))
 
     pl.semaphore_wait(barrier, expected)
+    for i in range(4):
+        when_sent(SIDES[i], lambda: setup_copy(i, True).start())
     for i in reversed(range(8)):
         when_sent(SIDES[i], lambda: setup_copy(i).start())
 
@@ -382,12 +386,13 @@
     ksend[pl.ds(52, 8), :] = lane_sum(ring[pl.ds(0, 8), :])
     ksend[pl.ds(60, 4), :] = jnp.zeros((4, LANES), jnp.float32)
 
-    def take(i):
-        when_there(SIDES[i], lambda: setup_copy(i).wait_recv())
-        unpack(SIDES[i], True, srecv, (i,), ext, fits(*SIDES[i]))
+    def take(i, first):
+        when_there(SIDES[i], lambda: setup_copy(i, first).wait_recv())
+        span = (0, 3) if first else (3 if i < 4 else 0, None)
+        unpack(SIDES[i], True, srecv, (i,), ext, fits(*SIDES[i]), *span)
 
     for i in range(4):
-        take(i)
+        take(i, True)
 
     def edge(axis, here, there):
         perm_here, _ = look_up(ext[MAT, here, :])
@@ -431,8 +436,8 @@
     for j in range(4):
         when_sent(NEAR[j], lambda: coef_copy(j).start())
 
-    for i in range(4, 8):
-        take(i)
+    for i in range(8):
+        take(i, False)
     look_up_rows(0, ROWS, 32)
     face_rows(0, 144, 24)
     for lo in range(16, 144, 16):
@@ -629,6 +634,8 @@
 
     for i, side in enumerate(SIDES):
         when_sent(side, lambda: setup_copy(i).wait_send())
+        if i < 4:
+            when_sent(side, lambda: setup_copy(i, True).wait_send())
     for i, side in enumerate(PARTNERS):
 
         def sent():
@@ -653,7 +660,7 @@
         n_part = len(PARTNERS)
         return pl.pallas_call(
             functools.partial(kernel, n_grp, n_sub),
-            out_shape=jax.ShapeDtypeStruct(cotangent.shape, jnp.float32),
+            out_shape=pltpu.VMEM(cotangent.shape, jnp.float32),
             in_specs=[hbm] * 6,
             out_specs=vmem,
             scratch_shapes=[
@@ -687,8 +694,8 @@
                 tile(4, 8),
                 tile(3, 4, 8),
                 dma((6,)),
-                dma((8,)),
-                dma((8,)),
+                dma((12,)),
+                dma((12,)),
                 dma((ROUNDS, n_part)),
                 dma((ROUNDS, n_part)),
                 dma((4,)),
@@ -697,7 +704,7 @@
             compiler_params=pltpu.CompilerParams(
                 collective_id=0, has_side_effects=True, vmem_limit_bytes=32 * 1024 * 1024
             ),
-        )(cotangent, head, materials, flags, perm_table, poro_table)
+        )(*(pltpu.with_memory_space_constraint(x, pltpu.HBM) for x in (cotangent, head, materials, flags, perm_table, poro_table)))
 
     return jax.shard_map(
         local,

time: 37.5 us -> 31.6 us (0.84)
  local copies, waits for them, and re-layouts: 5.19 us -> 0.63 us
  Pallas kernels: 32 us -> 30.8 us
    unnamed x13 -> x1, local copies, waits for them, and re-layouts: 5.19 us -> 0.63 us
    pallas_call x1, Pallas kernels: 32 us -> 30.8 us  [local(): pl.pallas_call(functools.partial(kernel, n_grp, n_sub), out_shape=pltpu.V...]
where the time goes in v2:
time: 31.6 us; the launch traced here: 31.5 us
  Pallas kernels  30.8 us (97%)
  local copies, waits for them, and re-layouts  0.63 us (2%)
    pallas_call x1, Pallas kernels, local(): pl.pallas_call(functools.partial(kernel, n_grp, n_sub), out_shape=pltpu.V...  30.8 us
    unnamed x1, local copies, waits for them, and re-layouts  0.63 us

profile of v2, /device:TPU:6, one launch (start us, length us, event | category | flops | bytes accessed | tf_op | source)
XLA Modules:
  0.0 31.5 jit_solution(7508467005311609908)
XLA Ops:
  0.0 30.8 %shard_map.64 = f32[2,8,8,128]{3,2,1,0:T(8,128)S(1)} custom-call(f32[2,8,8,128]{3,2,1,0:T(8,128)} %cot_hbm.1, f32[8,8,128]{2,1,0:T(8,128)} %head_hbm.1, s32[8,8,128]{2,1,0:T(8,128)} %mat_hbm.1, s32[3,8,8,128]{3,2,1,0:T(8,128)} %flag_hbm.1, f32[8]{0:T(128)} %perm_hbm.1, f32[8]{0:T(128)} %poro_hbm.1), custom_call_target="tpu_custom_call" | custom-call | tf_op jit(solution)/shard_map/pallas_call | solution.py:661
  30.8 0.6 %copy.8 = f32[2,8,8,128]{3,2,1,0:T(8,128)} copy(f32[2,8,8,128]{3,2,1,0:T(8,128)S(1)} %shard_map.64) | data formatting | bytes 131072

commit v3 on v1

--- a/solution.py
+++ b/solution.py
@@ -32,8 +32,11 @@
 TX, TXM, TY, TYM, TZ, TZM, SX, SXM, SY, SYM, SZ, SZM, BPP, BPC, BCP, BCC, IPP, IPC, ICP, ICC = range(20)
 N_COEF = 20
 N_CBLK = 13
-C_ROWS = 64
+N_INNER = 17
+C_ROWS = 120
+C_RAW = 40
 ROUNDS = ITERS - 1
+N_PART = 14
 
 
 def row(x, y):
@@ -49,13 +52,10 @@
 
 
 def setup_slots(low, along):
-    if low:
-        pairs = [(MAT, -2), (MAT, -1), (HEAD, -2), (HEAD, -1), (along, -2)]
-        one = -1
-    else:
-        pairs = [(MAT, 8), (MAT, 9), (HEAD, 8), (HEAD, 9)]
-        one = 8
-    return pairs + [(field, one) for field in (F0, F1, F2, COT, COT + 1)]
+    one, two = (-1, -2) if low else (8, 9)
+    first = [(MAT, one), (HEAD, one), (along, one)]
+    others = [(field, one) for field in (F0, F1, F2) if field != along]
+    return first + others + [(MAT, two), (HEAD, two)] + ([(along, two)] if low else []) + [(COT, one), (COT + 1, one)]
 
 
 def field_slots(low):
@@ -164,26 +164,24 @@
     srecv,
     rsend,
     rrecv,
+    xsend,
+    xrecv,
     ksend,
     krecv,
-    cagg,
+    cin,
+    cedge,
     ring,
     cco,
     cres,
     layer,
-    l_sem,
-    s_send,
-    s_recv,
-    r_send,
-    r_recv,
-    k_send,
-    k_recv,
+    sent,
+    came,
 ):
     g = lax.axis_index("grp")
     s = lax.axis_index("sub")
 
     def device(dx, dy):
-        return {"grp": lax.rem(g + dx + n_grp, n_grp), "sub": lax.rem(s + dy + n_sub, n_sub)}
+        return {"grp": g + dx, "sub": s + dy}
 
     def fits(dx, dy):
         found = []
@@ -195,7 +193,7 @@
         return found[0] if len(found) == 1 else jnp.logical_and(*found)
 
     loads = [
-        pltpu.make_async_copy(src, dst, l_sem.at[i])
+        pltpu.make_async_copy(src, dst, sent.at[i])
         for i, (src, dst) in enumerate((
             (mat_hbm, mat_ref), (head_hbm, head_ref), (flag_hbm, flag_ref), (cot_hbm, cot_ref), (perm_hbm, perm_tab), (poro_hbm, poro_tab)
         ))
@@ -225,22 +223,30 @@
 
     def setup_copy(i):
         dx, dy = SIDES[i]
-        part = pl.ds(0, rows_of((dx, dy), True))
+        part = pl.ds(0, rows_of((dx, dy), True) + (24 if i >= 4 else 0))
+        at = PARTNERS.index((dx, dy))
         return pltpu.make_async_remote_copy(
-            ssend.at[i, part], srecv.at[i, part], s_send.at[i], s_recv.at[i], device_id=device(-dx, -dy), device_id_type=MESH
+            ssend.at[i, part], srecv.at[i, part], sent.at[at], came.at[1, at], device_id=device(-dx, -dy), device_id_type=MESH
+        )
+
+    def edge_copy(i):
+        dx, dy = FAR[i]
+        return pltpu.make_async_remote_copy(
+            xsend.at[0 if dx < 0 else 1], xrecv.at[i], sent.at[i], came.at[1, i], device_id=device(-dx, -dy), device_id_type=MESH
         )
 
     def round_copy(i, k):
         dx, dy = PARTNERS[i]
         part = pl.ds(0, rows_of((dx, dy), False) + (16 if dx == 0 else 8))
         return pltpu.make_async_remote_copy(
-            rsend.at[k, i, part], rrecv.at[k, i, part], r_send.at[k, i], r_recv.at[k, i], device_id=device(-dx, -dy), device_id_type=MESH
+            rsend.at[k, i, part], rrecv.at[k, i, part], sent.at[i], came.at[lax.rem(k, 2), i], device_id=device(-dx, -dy), device_id_type=MESH
         )
 
     def coef_copy(j):
         dx, dy = NEAR[j]
+        at = PARTNERS.index((dx, dy)) if abs(dy) == 2 else N_PART + j - 2
         return pltpu.make_async_remote_copy(
-            ksend, krecv.at[j], k_send.at[j], k_recv.at[j], device_id=device(-dx, -dy), device_id_type=MESH
+            ksend, krecv.at[j], sent.at[at], came.at[1, at], device_id=device(-dx, -dy), device_id_type=MESH
         )
 
     def when_sent(side, act):
@@ -253,6 +259,29 @@
     ext[MAT] = zero_rows - 1.0
     for f in range(1, 7):
         ext[f] = zero_rows
+    for load in loads:
+        load.wait()
+    for x in range(8):
+        ext[MAT, rows(x, 0), :] = mat_ref[x].astype(jnp.float32)
+        ext[HEAD, rows(x, 0), :] = head_ref[x]
+        for d in range(3):
+            ext[F0 + d, rows(x, 0), :] = flag_ref[d, x].astype(jnp.float32)
+        for f in range(2):
+            ext[COT + f, rows(x, 0), :] = cot_ref[f, x]
+    for i, x in enumerate((7, 0)):
+        for m, field in enumerate((MAT, HEAD, F0)):
+            xsend[i, pl.ds(8 * m, 8), :] = ext[field, rows(x, 0), :]
+    for i, side in enumerate(SIDES):
+        pack(side, True, ext, ssend, (i,))
+        if i >= 4:
+            ssend[i, pl.ds(24, 24), :] = xsend[0 if side[0] < 0 else 1]
+
+    pl.semaphore_wait(barrier, expected)
+    for i in reversed(range(8)):
+        when_sent(SIDES[i], lambda: setup_copy(i).start())
+    for i in range(4):
+        when_sent(FAR[i], lambda: edge_copy(i).start())
+
     mask[...] = zero_rows
     perm[...] = zero_rows
     poro[...] = zero_rows
@@ -265,40 +294,6 @@
         face[m, pl.ds(0, 32), :] = jnp.zeros((32, LANES), jnp.float32)
     for x in range(-1, 9):
         mask[rows(x, -1, 10), :] = jnp.ones((10, LANES), jnp.float32)
-    for i, side in enumerate(SIDES):
-
-        @pl.when(jnp.logical_not(fits(*side)))
-        def _():
-            srecv[i] = jnp.zeros((80, LANES), jnp.float32)
-
-    for i, side in enumerate(PARTNERS):
-
-        @pl.when(jnp.logical_not(fits(*side)))
-        def _():
-            for k in range(ROUNDS):
-                rrecv[k, i] = jnp.zeros((48, LANES), jnp.float32)
-
-    for j, side in enumerate(NEAR):
-
-        @pl.when(jnp.logical_not(fits(*side)))
-        def _():
-            krecv[j] = jnp.zeros((C_ROWS, LANES), jnp.float32)
-
-    for load in loads:
-        load.wait()
-    for x in range(8):
-        ext[MAT, rows(x, 0), :] = mat_ref[x].astype(jnp.float32)
-        ext[HEAD, rows(x, 0), :] = head_ref[x]
-        for d in range(3):
-            ext[F0 + d, rows(x, 0), :] = flag_ref[d, x].astype(jnp.float32)
-        for f in range(2):
-            ext[COT + f, rows(x, 0), :] = cot_ref[f, x]
-    for i, side in enumerate(SIDES):
-        pack(side, True, ext, ssend, (i,))
-
-    pl.semaphore_wait(barrier, expected)
-    for i in reversed(range(8)):
-        when_sent(SIDES[i], lambda: setup_copy(i).start())
 
     def look_up(mats):
         perm_here = jnp.zeros_like(mats)
@@ -339,100 +334,66 @@
     look_up_rows(32, 128, 32)
     face_rows(32, 128, 24)
 
-    def put(block, cx, cy, value):
-        cagg[pl.ds(4 * block + 2 * cx + cy, 1), :] = value
-
-    def put_y(block, cx, value):
+    def put(ref, at, value):
         value = four_sum(value)
-        put(block, cx, 0, value[0:1])
-        put(block, cx, 1, value[4:5])
-
-    def put_x(block, cy, value):
-        value = four_sum(value)
-        put(block, 0, cy, value[0:1])
-        put(block, 1, cy, value[4:5])
-
-    cagg[...] = jnp.zeros((64, LANES), jnp.float32)
+        ref[pl.ds(at, 1), :] = value[0:1]
+        ref[pl.ds(at + 1, 1), :] = value[4:5]
+
     lane = lax.broadcasted_iota(jnp.int32, (8, LANES), 1)
     for cx in range(2):
-        sums = [0.0] * 5
+        sums = [0.0] * 7
         for x in range(4 * cx, 4 * cx + 4):
             here = rows(x, 0)
             zs = [face[6 + m, here, :] for m in range(3)]
             out = face[1, here, :] + face[4, here, :] + zs[1]
             out = out + face[2, rows(x - 1, 0), :] + face[5, rows(x, -1), :] + last_lane(zs[2])
-            sums = [old + new for old, new in zip(sums, [poro[here, :], out] + zs)]
+            news = [poro[here, :], out] + zs + [ext[COT + f, here, :] for f in range(2)]
+            sums = [old + new for old, new in zip(sums, news)]
         for m in range(2, 5):
             sums[m] = jnp.where(lane % AGG == AGG - 1, sums[m], 0.0)
-        for b, value in zip((0, 1, 12, 13, 14), sums):
-            put_y(b, cx, value)
-    for b, cx, m in ((2, 0, 0), (3, 1, 0), (4, 0, 1), (5, 0, 2), (6, 1, 2)):
-        put_y(b, cx, face[m, rows(3, 0), :])
-    for b, cy, m in ((7, 0, 0), (8, 1, 0), (9, 0, 1), (10, 0, 2), (11, 1, 2)):
-        put_x(b, cy, face[3 + m, column(3), :])
-    for f in range(2):
-        for cx in range(2):
-            total = ext[COT + f, rows(4 * cx, 0), :]
-            for x in range(4 * cx + 1, 4 * cx + 4):
-                total = total + ext[COT + f, rows(x, 0), :]
-            total = four_sum(total)
-            first = 4 * f + 2 * cx
-            ring[pl.ds(first, 1), :] = total[0:1]
-            ring[pl.ds(first + 1, 1), :] = total[4:5]
-    ksend[pl.ds(52, 8), :] = lane_sum(ring[pl.ds(0, 8), :])
-    ksend[pl.ds(60, 4), :] = jnp.zeros((4, LANES), jnp.float32)
-
-    def take(i):
-        when_there(SIDES[i], lambda: setup_copy(i).wait_recv())
-        unpack(SIDES[i], True, srecv, (i,), ext, fits(*SIDES[i]))
-
-    for i in range(4):
-        take(i)
-
-    def edge(axis, here, there):
-        perm_here, _ = look_up(ext[MAT, here, :])
-        perm_next, _ = look_up(ext[MAT, there, :])
-        return one_face(perm_here, ext[HEAD, here, :], perm_next, ext[HEAD, there, :], ext[F0 + axis, here, :])
-
-    trans, _, lower = edge(0, rows(-1, 0), rows(0, 0))
-    put_y(3, 0, trans)
-    put_y(6, 0, lower)
-    trans, upper, _ = edge(0, rows(7, 0), rows(8, 0))
-    put_y(2, 1, trans)
-    put_y(4, 1, upper)
-    trans, _, lower = edge(1, column(-1), column(0))
-    put_x(8, 0, trans)
-    put_x(11, 0, lower)
-    trans, upper, lower = edge(1, column(7), column(8))
-    put_x(7, 1, trans)
-    put_x(9, 1, upper)
-    put_x(10, 1, lower)
-    cagg[...] = lane_sum(cagg[...])
-
-    def block(b):
-        return cagg[pl.ds(4 * b, 4), :]
-
-    place = lax.broadcasted_iota(jnp.int32, (4, LANES), 0)
-    store = block(0)
-    t_z, a_z, b_z = block(12), block(13), block(14)
-    edge_sum = block(2) + block(3) + block(7) + block(8) + t_z + last_lane(t_z, AGG)
-    edge_out = block(4) + block(6) + block(9) + block(11) + a_z + last_lane(b_z, AGG)
-    out = block(1) + jnp.where(place < 2, block(6), block(4)) + jnp.where(place % 2 == 0, block(11), block(9))
-    cpp, cpc, ccp, ccc = store + edge_sum, -CPL_S * out, CPL_P * store, store + DISP * edge_sum + edge_out
-    scale = OMEGA_C / (cpp * ccc - cpc * ccp)
-    t_x, t_y = block(2), block(7)
-    for b, value in enumerate((
-        ccc * scale, -cpc * scale, -ccp * scale, cpp * scale,
-        t_y, DISP * t_y + block(9), DISP * t_y + block(10),
-        t_z, DISP * t_z + a_z, DISP * t_z + b_z,
-        t_x, DISP * t_x + block(4), DISP * t_x + block(5),
-    )):
-        ksend[pl.ds(4 * b, 4), :] = value
+        for item, value in zip((0, 2, 4, 6, 8, 13, 15), sums):
+            put(ksend, 2 * (item + cx), value)
+    for m in range(3):
+        put(ksend, 2 * (10 + m), face[m, rows(3, 0), :])
+        put(ksend, 2 * (17 + m), face[3 + m, column(3), :])
+    ksend[pl.ds(0, C_RAW), :] = lane_sum(ksend[pl.ds(0, C_RAW), :])
+    raw = [
+        (MAT, rows(0, 0)), (HEAD, rows(0, 0)), (MAT, rows(7, 0)), (HEAD, rows(7, 0)), (F0, rows(7, 0)),
+        (MAT, column(0)), (HEAD, column(0)), (MAT, column(7)), (HEAD, column(7)), (F1, column(7)),
+    ]
+    for slot, (field, where) in enumerate(raw):
+        ksend[pl.ds(C_RAW + 8 * slot, 8), :] = ext[field, where, :]
     for j in range(4):
         when_sent(NEAR[j], lambda: coef_copy(j).start())
 
-    for i in range(4, 8):
-        take(i)
+    for i, side in enumerate(SIDES):
+
+        @pl.when(jnp.logical_not(fits(*side)))
+        def _():
+            srecv[i] = jnp.zeros((80, LANES), jnp.float32)
+
+    for i, side in enumerate(PARTNERS):
+
+        @pl.when(jnp.logical_not(fits(*side)))
+        def _():
+            for k in range(ROUNDS):
+                rrecv[k, i] = jnp.zeros((48, LANES), jnp.float32)
+
+    for j, side in enumerate(NEAR):
+
+        @pl.when(jnp.logical_not(fits(*side)))
+        def _():
+            krecv[j] = jnp.zeros((C_ROWS, LANES), jnp.float32)
+
+    for j, side in enumerate(FAR[:4]):
+
+        @pl.when(jnp.logical_not(fits(*side)))
+        def _():
+            xrecv[j] = jnp.zeros((24, LANES), jnp.float32)
+
+    for i, side in enumerate(SIDES):
+        when_there(side, lambda: setup_copy(i).wait_recv())
+        unpack(side, True, srecv, (i,), ext, fits(*side))
     look_up_rows(0, ROWS, 32)
     face_rows(0, 144, 24)
     for lo in range(16, 144, 16):
@@ -570,6 +531,8 @@
 
     def receive(k):
         for i, side in enumerate(PARTNERS):
+            when_sent(side, lambda: round_copy(i, k).wait_send())
+        for i, side in enumerate(PARTNERS):
             when_there(side, lambda: round_copy(i, k).wait_recv())
             if side not in FAR:
                 unpack(side, False, rrecv, (k, i), adj, None)
@@ -600,21 +563,103 @@
 
     fine_solve(ext, COT)
 
+    for i, side in enumerate(SIDES):
+        when_sent(side, lambda: setup_copy(i).wait_send())
+    for j, side in enumerate(NEAR):
+        when_sent(side, lambda: coef_copy(j).wait_send())
+        when_sent(FAR[j], lambda: edge_copy(j).wait_send())
     for j in range(4):
         when_there(NEAR[j], lambda: coef_copy(j).wait_recv())
-    for item in range(2 * N_CBLK + 4):
-
-        def put_coarse(where, value):
-            if item < 2 * N_CBLK:
-                cco[item // 2, item % 2, where, :] = value
+        when_there(FAR[j], lambda: edge_copy(j).wait_recv())
+
+    def near(u):
+        return NEAR.index((0, u))
+
+    def inner(u, at, count):
+        return (ksend[pl.ds(at, count), :] if u == 0 else krecv[near(u), pl.ds(at, count), :])
+
+    def raw_of(u, slot):
+        value = inner(u, C_RAW + 8 * slot, 8)
+        return jnp.where(fits(0, u), value, -1.0) if u != 0 and slot in (0, 2, 5, 7) else value
+
+    def beyond(dx, u, m):
+        if u == 0:
+            return ext[(MAT, HEAD, F0)[m], rows(-1 if dx < 0 else 8, 0), :]
+        if abs(u) == 1:
+            value = srecv[SIDES.index((dx, u)), pl.ds(24 + 8 * m, 8), :]
+        else:
+            value = xrecv[FAR.index((dx, u)), pl.ds(8 * m, 8), :]
+        return jnp.where(fits(dx, u), value, -1.0) if m == 0 else value
+
+    def between(mat_a, head_a, flag, mat_b, head_b):
+        return one_face(look_up(mat_a)[0], head_a, look_up(mat_b)[0], head_b, flag)
+
+    def put_rows(tile, u, value):
+        value = four_sum(value)
+        if u > -2:
+            cedge[tile, pl.ds(2 * u + 3, 1), :] = value[0:1]
+        if u < 2:
+            cedge[tile, pl.ds(2 * u + 4, 1), :] = value[4:5]
+
+    for tile in range(4, 10):
+        cedge[tile] = jnp.zeros((8, LANES), jnp.float32)
+    for u in range(-2, 3):
+        trans, _, lower = between(*(beyond(-1, u, m) for m in range(3)), raw_of(u, 0), raw_of(u, 1))
+        put_rows(0, u, trans)
+        put_rows(1, u, lower)
+        trans, upper, _ = between(raw_of(u, 2), raw_of(u, 3), raw_of(u, 4), beyond(1, u, 0), beyond(1, u, 1))
+        put_rows(2, u, trans)
+        put_rows(3, u, upper)
+        if u < 2:
+            values = between(raw_of(u, 7), raw_of(u, 8), raw_of(u, 9), raw_of(u + 1, 5), raw_of(u + 1, 6))
+            for m in range(3):
+                value = four_sum(values[m])
+                for cx in range(2):
+                    cedge[4 + 2 * m + cx, pl.ds(2 * u + 4, 1), :] = value[4 * cx : 4 * cx + 1]
+    for tile in range(10):
+        cedge[tile] = lane_sum(cedge[tile])
+    for m in range(3):
+        for cx in range(2):
+            for u in range(-1, 3):
+                cedge[4 + 2 * m + cx, pl.ds(2 * u + 3, 1), :] = inner(u, 34 + 2 * m + cx, 1)
+    for item in range(N_INNER):
+
+        def put_inner(where, value):
+            if item < 13:
+                cin[item, where, :] = value
             else:
-                cres[item - 2 * N_CBLK, where, :] = value
-
-        put_coarse(pl.ds(0, 1), krecv[0, pl.ds(2 * item + 1, 1), :])
-        put_coarse(pl.ds(1, 2), krecv[2, pl.ds(2 * item, 2), :])
-        put_coarse(pl.ds(3, 2), ksend[pl.ds(2 * item, 2), :])
-        put_coarse(pl.ds(5, 2), krecv[3, pl.ds(2 * item, 2), :])
-        put_coarse(pl.ds(7, 1), krecv[1, pl.ds(2 * item, 1), :])
+                cres[item - 13, where, :] = value
+
+        put_inner(pl.ds(0, 1), inner(-2, 2 * item + 1, 1))
+        put_inner(pl.ds(1, 2), inner(-1, 2 * item, 2))
+        put_inner(pl.ds(3, 2), inner(0, 2 * item, 2))
+        put_inner(pl.ds(5, 2), inner(1, 2 * item, 2))
+        put_inner(pl.ds(7, 1), inner(2, 2 * item, 1))
+
+    place = lax.broadcasted_iota(jnp.int32, (8, LANES), 0)
+    m_t, m_a, m_b = (cin[10 + m] for m in range(3))
+    for cx in range(2):
+        store, out, t_z, a_z, b_z = (cin[2 * m + cx] for m in range(5))
+        t_y, a_y, b_y = (cedge[4 + 2 * m + cx] for m in range(3))
+        under_t, under_b = (
+            jnp.where(place == 0, jnp.broadcast_to(inner(-2, 34 + 2 * m + cx, 1), (8, LANES)), pltpu.roll(value, 1, 0))
+            for m, value in ((0, t_y), (2, b_y))
+        )
+        side_t, side_out = (cedge[0], cedge[1]) if cx == 0 else (cedge[2], cedge[3])
+        edge_sum = m_t + side_t + t_y + under_t + t_z + last_lane(t_z, AGG)
+        edge_out = (m_a if cx == 0 else m_b) + side_out + a_y + under_b + a_z + last_lane(b_z, AGG)
+        out = out + side_out + jnp.where(place % 2 == 0, a_y, under_b)
+        cpp, cpc, ccp, ccc = store + edge_sum, -CPL_S * out, CPL_P * store, store + DISP * edge_sum + edge_out
+        inside = cpp > 0.0
+        determ = jnp.where(inside, cpp * ccc - cpc * ccp, 1.0)
+        scale = jnp.where(inside, OMEGA_C / determ, 0.0)
+        for b, value in enumerate((
+            ccc * scale, -cpc * scale, -ccp * scale, cpp * scale,
+            t_y, DISP * t_y + a_y, DISP * t_y + b_y,
+            t_z, DISP * t_z + a_z, DISP * t_z + b_z,
+            m_t, DISP * m_t + m_a, DISP * m_t + m_b,
+        )):
+            cco[b, cx] = value
     update()
     send(0)
 
@@ -627,18 +672,6 @@
 
     lax.fori_loop(1, ITERS, step, 0)
 
-    for i, side in enumerate(SIDES):
-        when_sent(side, lambda: setup_copy(i).wait_send())
-    for i, side in enumerate(PARTNERS):
-
-        def sent():
-            for k in range(ROUNDS):
-                round_copy(i, k).wait_send()
-
-        when_sent(side, sent)
-    for j, side in enumerate(NEAR):
-        when_sent(side, lambda: coef_copy(j).wait_send())
-
 
 def solution(mesh):
     n_grp, n_sub = mesh.shape["grp"], mesh.shape["sub"]
@@ -650,10 +683,9 @@
         dma = pltpu.SemaphoreType.DMA
         vmem = pl.BlockSpec(memory_space=pltpu.VMEM)
         hbm = pl.BlockSpec(memory_space=pltpu.HBM)
-        n_part = len(PARTNERS)
         return pl.pallas_call(
             functools.partial(kernel, n_grp, n_sub),
-            out_shape=jax.ShapeDtypeStruct(cotangent.shape, jnp.float32),
+            out_shape=pltpu.VMEM(cotangent.shape, jnp.float32),
             in_specs=[hbm] * 6,
             out_specs=vmem,
             scratch_shapes=[
@@ -677,27 +709,25 @@
                 tile(2, ROWS),
                 tile(8, 80),
                 tile(8, 80),
-                tile(ROUNDS, n_part, 48),
-                tile(ROUNDS, n_part, 48),
+                tile(ROUNDS, N_PART, 48),
+                tile(ROUNDS, N_PART, 48),
+                tile(2, 24),
+                tile(4, 24),
                 tile(C_ROWS),
                 tile(4, C_ROWS),
-                tile(64),
+                tile(13, 8),
+                tile(10, 8),
                 tile(24),
                 tile(N_CBLK, 2, 8),
                 tile(4, 8),
                 tile(3, 4, 8),
-                dma((6,)),
-                dma((8,)),
-                dma((8,)),
-                dma((ROUNDS, n_part)),
-                dma((ROUNDS, n_part)),
-                dma((4,)),
-                dma((4,)),
+                dma((N_PART + 2,)),
+                dma((2, N_PART + 2)),
             ],
             compiler_params=pltpu.CompilerParams(
                 collective_id=0, has_side_effects=True, vmem_limit_bytes=32 * 1024 * 1024
             ),
-        )(cotangent, head, materials, flags, perm_table, poro_table)
+        )(*(pltpu.with_memory_space_constraint(x, pltpu.HBM) for x in (cotangent, head, materials, flags, perm_table, poro_table)))
 
     return jax.shard_map(
         local,

time: 37.5 us -> 30.3 us (0.81)
  local copies, waits for them, and re-layouts: 5.19 us -> 0.63 us
  Pallas kernels: 32 us -> 29.6 us
    unnamed x13 -> x1, local copies, waits for them, and re-layouts: 5.19 us -> 0.63 us
    pallas_call x1, Pallas kernels: 32 us -> 29.6 us  [local(): pl.pallas_call(functools.partial(kernel, n_grp, n_sub), out_shape=pltpu.V...]
where the time goes in v3:
time: 30.3 us; the launch traced here: 30.2 us
  Pallas kernels  29.6 us (98%)
  local copies, waits for them, and re-layouts  0.63 us (2%)
    pallas_call x1, Pallas kernels, local(): pl.pallas_call(functools.partial(kernel, n_grp, n_sub), out_shape=pltpu.V...  29.6 us
    unnamed x1, local copies, waits for them, and re-layouts  0.63 us

profile of v3, /device:TPU:6, one launch (start us, length us, event | category | flops | bytes accessed | tf_op | source)
XLA Modules:
  0.0 30.2 jit_solution(17944521607705328534)
XLA Ops:
  0.0 29.6 %shard_map.64 = f32[2,8,8,128]{3,2,1,0:T(8,128)S(1)} custom-call(f32[2,8,8,128]{3,2,1,0:T(8,128)} %cot_hbm.1, f32[8,8,128]{2,1,0:T(8,128)} %head_hbm.1, s32[8,8,128]{2,1,0:T(8,128)} %mat_hbm.1, s32[3,8,8,128]{3,2,1,0:T(8,128)} %flag_hbm.1, f32[8]{0:T(128)} %perm_hbm.1, f32[8]{0:T(128)} %poro_hbm.1), custom_call_target="tpu_custom_call" | custom-call | tf_op jit(solution)/shard_map/pallas_call | solution.py:686
  29.6 0.6 %copy.8 = f32[2,8,8,128]{3,2,1,0:T(8,128)} copy(f32[2,8,8,128]{3,2,1,0:T(8,128)S(1)} %shard_map.64) | data formatting | bytes 131072

commit v4 on v3

--- a/solution.py
+++ b/solution.py
@@ -31,10 +31,12 @@
 MAT, HEAD, F0, F1, F2, COT = 0, 1, 2, 3, 4, 5
 TX, TXM, TY, TYM, TZ, TZM, SX, SXM, SY, SYM, SZ, SZM, BPP, BPC, BCP, BCC, IPP, IPC, ICP, ICC = range(20)
 N_COEF = 20
-N_CBLK = 13
+N_CBLK = 14
 N_INNER = 17
 C_ROWS = 120
 C_RAW = 40
+PAD = 40
+R_ROWS = 64
 ROUNDS = ITERS - 1
 N_PART = 14
 
@@ -69,18 +71,18 @@
     return setup_slots(dy < 0, F1) if setup else field_slots(dy < 0)
 
 
-def pack(side, setup, src, dst, lead):
+def pack(side, setup, src, dst, lead, base=0):
     dx, dy = side
     for slot, (field, layer) in enumerate(slots_of(side, setup)):
         if dy == 0:
-            dst[lead + (pl.ds(8 * slot, 8),)] = src[field, rows(layer % 8, 0), :]
+            dst[lead + (pl.ds(base + 8 * slot, 8),)] = src[field, rows(layer % 8, 0), :]
         elif dx == 0:
-            dst[lead + (pl.ds(8 * slot, 8),)] = src[field, column(layer % 8), :]
+            dst[lead + (pl.ds(base + 8 * slot, 8),)] = src[field, column(layer % 8), :]
         else:
-            dst[lead + (pl.ds(2 * slot, 2),)] = src[field, rows(layer % 8, 6 if dy < 0 else 0, 2), :]
-
-
-def unpack(side, setup, src, lead, dst, valid):
+            dst[lead + (pl.ds(base + 2 * slot, 2),)] = src[field, rows(layer % 8, 6 if dy < 0 else 0, 2), :]
+
+
+def unpack(side, setup, src, lead, dst, valid, base=0):
     dx, dy = side
 
     def seen(field, value):
@@ -88,11 +90,11 @@
 
     for slot, (field, layer) in enumerate(slots_of(side, setup)):
         if dy == 0:
-            dst[field, rows(layer, 0), :] = seen(field, src[lead + (pl.ds(8 * slot, 8),)])
+            dst[field, rows(layer, 0), :] = seen(field, src[lead + (pl.ds(base + 8 * slot, 8),)])
         elif dx == 0:
-            dst[field, column(layer), :] = seen(field, src[lead + (pl.ds(8 * slot, 8),)])
+            dst[field, column(layer), :] = seen(field, src[lead + (pl.ds(base + 8 * slot, 8),)])
         else:
-            dst[field, rows(layer, -2 if dy < 0 else 8, 2), :] = seen(field, src[lead + (pl.ds(2 * slot, 2),)])
+            dst[field, rows(layer, -2 if dy < 0 else 8, 2), :] = seen(field, src[lead + (pl.ds(base + 2 * slot, 2),)])
 
 
 def next_lane(value, by=1):
@@ -105,11 +107,8 @@
 
 def lane_sum(value):
     lane = lax.broadcasted_iota(jnp.int32, value.shape, 1)
-    total = value + next_lane(value)
-    total = total + next_lane(total, 2)
-    total = jnp.where(lane % AGG == 0, total, 0.0)
-    total = total + last_lane(total)
-    return total + last_lane(total, 2)
+    total = value + jnp.where(lane % 2 == 0, next_lane(value), last_lane(value))
+    return total + jnp.where(lane % AGG < 2, next_lane(total, 2), last_lane(total, 2))
 
 
 def four_sum(value):
@@ -173,7 +172,6 @@
     ring,
     cco,
     cres,
-    layer,
     sent,
     came,
 ):
@@ -237,7 +235,8 @@
 
     def round_copy(i, k):
         dx, dy = PARTNERS[i]
-        part = pl.ds(0, rows_of((dx, dy), False) + (16 if dx == 0 else 8))
+        halo = rows_of((dx, dy), False)
+        part = pl.ds(PAD - halo, halo + (16 if dx == 0 else 8))
         return pltpu.make_async_remote_copy(
             rsend.at[k, i, part], rrecv.at[k, i, part], sent.at[i], came.at[lax.rem(k, 2), i], device_id=device(-dx, -dy), device_id_type=MESH
         )
@@ -377,7 +376,7 @@
         @pl.when(jnp.logical_not(fits(*side)))
         def _():
             for k in range(ROUNDS):
-                rrecv[k, i] = jnp.zeros((48, LANES), jnp.float32)
+                rrecv[k, i] = jnp.zeros((R_ROWS, LANES), jnp.float32)
 
     for j, side in enumerate(NEAR):
 
@@ -442,35 +441,25 @@
             fin[1, here, :] = (1.0 - OMEGA) * z_c + grd[1, here, :] + co[ICP, here, :] * s_p + co[ICC, here, :] * s_c
 
     def coarse_solve():
-        ipp, ipc, icp, icc = ([cco[b, cx] for cx in range(2)] for b in range(4))
-        t_y, a_y, b_y, t_z, a_z, b_z = ([cco[b, cx] for cx in range(2)] for b in range(4, 10))
-        t_x, a_x, b_x = (cco[b, 0] for b in range(10, 13))
-        ahead = {0: (t_y, t_z), 1: (a_y, a_z)}
-        behind = {
-            0: ([pltpu.roll(v, 1, 0) for v in t_y], [last_lane(v, AGG) for v in t_z]),
-            1: ([pltpu.roll(v, 1, 0) for v in b_y], [last_lane(v, AGG) for v in b_z]),
-        }
-        across = {0: (t_x, t_x), 1: (a_x, b_x)}
+        inv = [[cco[b, cx] for cx in range(2)] for b in range(4)]
         r = [[cres[2 * f + cx] for cx in range(2)] for f in range(2)]
-        base = [
-            [ipp[cx] * r[0][cx] + ipc[cx] * r[1][cx] for cx in range(2)],
-            [icp[cx] * r[0][cx] + icc[cx] * r[1][cx] for cx in range(2)],
-        ]
+
+        def inverse(v):
+            return [[inv[2 * f][cx] * v[0][cx] + inv[2 * f + 1][cx] * v[1][cx] for cx in range(2)] for f in range(2)]
+
+        base = inverse(r)
         z = base
         for sweep in range(3):
             acc = [[None] * 2 for f in range(2)]
             for f in range(2):
                 for cx in range(2):
                     v = z[f][cx]
-                    total = across[f][cx] * z[f][1 - cx]
-                    total = total + ahead[f][0][cx] * pltpu.roll(v, 7, 0)
-                    total = total + behind[f][0][cx] * pltpu.roll(v, 1, 0)
-                    total = total + ahead[f][1][cx] * next_lane(v, AGG)
-                    acc[f][cx] = total + behind[f][1][cx] * last_lane(v, AGG)
-            z = [
-                [(1.0 - OMEGA_C) * z[0][cx] + base[0][cx] + ipp[cx] * acc[0][cx] + ipc[cx] * acc[1][cx] for cx in range(2)],
-                [(1.0 - OMEGA_C) * z[1][cx] + base[1][cx] + icp[cx] * acc[0][cx] + icc[cx] * acc[1][cx] for cx in range(2)],
-            ]
+                    first = 4 + 5 * f
+                    along = cco[first, cx] * pltpu.roll(v, 7, 0) + cco[first + 1, cx] * pltpu.roll(v, 1, 0)
+                    down = cco[first + 2, cx] * next_lane(v, AGG) + cco[first + 3, cx] * last_lane(v, AGG)
+                    acc[f][cx] = cco[first + 4, cx] * z[f][1 - cx] + (along + down)
+            more = inverse(acc)
+            z = [[((1.0 - OMEGA_C) * z[f][cx] + base[f][cx]) + more[f][cx] for cx in range(2)] for f in range(2)]
         upper = lax.broadcasted_iota(jnp.int32, (8, LANES), 0) < AGG
         return [
             [
@@ -499,7 +488,7 @@
             res[1, here, :] = co[BCP, here, :] * z_p + co[BCC, here, :] * z_c - s_c
 
         def place(at, value):
-            ring[pl.ds(at, 1), :] = value
+            ring[pl.ds(8 + at, 1), :] = value
 
         for f in range(2):
             for cx in range(2):
@@ -517,16 +506,16 @@
                 total = four_sum(res[f, rows(x, 0), :])
                 place(at + 2 * f, total[0:1])
                 place(at + 2 * f + 1, total[4:5])
-        ring[...] = lane_sum(ring[...])
-        along, beside = ring[pl.ds(0, 16), :], ring[pl.ds(16, 8), :]
+        sums = lane_sum(ring[pl.ds(8, 24), :])
+        ring[pl.ds(8, 24), :] = sums
+        along, beside = sums[0:16], sums[16:24]
         for i, side in enumerate(PARTNERS):
             if side not in FAR:
-                pack(side, False, adj, rsend, (k, i))
-            at = rows_of(side, False)
+                pack(side, False, adj, rsend, (k, i), PAD - rows_of(side, False))
             if side[0] == 0:
-                rsend[k, i, pl.ds(at, 16), :] = along
+                rsend[k, i, pl.ds(PAD, 16), :] = along
             else:
-                rsend[k, i, pl.ds(at, 8), :] = beside
+                rsend[k, i, pl.ds(PAD, 8), :] = beside
             when_sent(side, lambda: round_copy(i, k).start())
 
     def receive(k):
@@ -535,26 +524,25 @@
         for i, side in enumerate(PARTNERS):
             when_there(side, lambda: round_copy(i, k).wait_recv())
             if side not in FAR:
-                unpack(side, False, rrecv, (k, i), adj, None)
+                unpack(side, False, rrecv, (k, i), adj, None, PAD - rows_of(side, False))
+        at_row = lax.broadcasted_iota(jnp.int32, (8, LANES), 0)
         for f in range(2):
             for cx in range(2):
                 item = 2 * f + cx
 
-                def along(dy, first, count):
-                    i = PARTNERS.index((0, dy))
-                    return rrecv[k, i, pl.ds(rows_of((0, dy), False) + 4 * item + first, count), :]
-
-                layer[0, item, pl.ds(0, 4), :] = along(-1, 0, 4)
-                layer[0, item, pl.ds(4, 4), :] = along(1, 0, 4)
-                layer[1, item, pl.ds(0, 2), :] = along(-2, 2, 2)
-                layer[1, item, pl.ds(2, 4), :] = ring[pl.ds(4 * item, 4), :]
-                layer[1, item, pl.ds(6, 2), :] = along(2, 0, 2)
-                dx = 2 * cx - 1
-                for dy in range(-2, 3):
-                    first, count = max(2 * dy + 3, 0), 1 if abs(dy) == 2 else 2
-                    at = rows_of((dx, dy), False) + (4 if dx < 0 else 0) + 2 * f + (1 if dy == -2 else 0)
-                    layer[2, item, pl.ds(first, count), :] = rrecv[k, PARTNERS.index((dx, dy)), pl.ds(at, count), :]
-                cres[item] = cres[item] - layer[0, item] - layer[1, item] - layer[2, item]
+                def along(dy, shift):
+                    return rrecv[k, PARTNERS.index((0, dy)), pl.ds(PAD + 4 * item + shift, 8), :]
+
+                def beside(dy):
+                    dx = 2 * cx - 1
+                    at = PAD + (4 if dx < 0 else 0) + 2 * f
+                    return rrecv[k, PARTNERS.index((dx, dy)), pl.ds(at - 2 * dy - 3, 8), :]
+
+                one = jnp.where(at_row < 4, along(-1, 0), along(1, -4))
+                two = jnp.where(at_row < 2, along(-2, 2), jnp.where(at_row < 6, ring[pl.ds(8 + 4 * item - 2, 8), :], along(2, -6)))
+                three = jnp.where(at_row < 1, beside(-2), jnp.where(at_row < 3, beside(-1), beside(0)))
+                three = jnp.where(at_row < 5, three, jnp.where(at_row < 7, beside(1), beside(2)))
+                cres[item] = cres[item] - ((one + two) + three)
         for lo in range(16, 144, 16):
             here = pl.ds(lo, 16)
             z_p, s_p, z_c, s_c = couple(co, adj, lo, 16)
@@ -655,9 +643,9 @@
         scale = jnp.where(inside, OMEGA_C / determ, 0.0)
         for b, value in enumerate((
             ccc * scale, -cpc * scale, -ccp * scale, cpp * scale,
-            t_y, DISP * t_y + a_y, DISP * t_y + b_y,
-            t_z, DISP * t_z + a_z, DISP * t_z + b_z,
-            m_t, DISP * m_t + m_a, DISP * m_t + m_b,
+            t_y, pltpu.roll(t_y, 1, 0), t_z, last_lane(t_z, AGG), m_t,
+            DISP * t_y + a_y, pltpu.roll(DISP * t_y + b_y, 1, 0), DISP * t_z + a_z, last_lane(DISP * t_z + b_z, AGG),
+            DISP * m_t + (m_a if cx == 0 else m_b),
         )):
             cco[b, cx] = value
     update()
@@ -709,18 +697,17 @@
                 tile(2, ROWS),
                 tile(8, 80),
                 tile(8, 80),
-                tile(ROUNDS, N_PART, 48),
-                tile(ROUNDS, N_PART, 48),
+                tile(ROUNDS, N_PART, R_ROWS),
+                tile(ROUNDS, N_PART, R_ROWS),
                 tile(2, 24),
                 tile(4, 24),
                 tile(C_ROWS),
                 tile(4, C_ROWS),
                 tile(13, 8),
                 tile(10, 8),
-                tile(24),
+                tile(32),
                 tile(N_CBLK, 2, 8),
                 tile(4, 8),
-                tile(3, 4, 8),
                 dma((N_PART + 2,)),
                 dma((2, N_PART + 2)),
             ],

time: 30.3 us -> 29.7 us (0.980)
  Pallas kernels: 29.6 us -> 29 us
    pallas_call x1, Pallas kernels: 29.6 us -> 29 us  [local(): pl.pallas_call(functools.partial(kernel, n_grp, n_sub), out_shape=pltpu.V...]
where the time goes in v4:
time: 29.7 us; the launch traced here: 29.6 us
  Pallas kernels  29 us (98%)
  local copies, waits for them, and re-layouts  0.63 us (2%)
    pallas_call x1, Pallas kernels, local(): pl.pallas_call(functools.partial(kernel, n_grp, n_sub), out_shape=pltpu.V...  29 us
    unnamed x1, local copies, waits for them, and re-layouts  0.63 us

profile of v4, /device:TPU:6, one launch (start us, length us, event | category | flops | bytes accessed | tf_op | source)
XLA Modules:
  0.0 29.6 jit_solution(14275841698912028661)
XLA Ops:
  0.0 29.0 %shard_map.64 = f32[2,8,8,128]{3,2,1,0:T(8,128)S(1)} custom-call(f32[2,8,8,128]{3,2,1,0:T(8,128)} %cot_hbm.1, f32[8,8,128]{2,1,0:T(8,128)} %head_hbm.1, s32[8,8,128]{2,1,0:T(8,128)} %mat_hbm.1, s32[3,8,8,128]{3,2,1,0:T(8,128)} %flag_hbm.1, f32[8]{0:T(128)} %perm_hbm.1, f32[8]{0:T(128)} %poro_hbm.1), custom_call_target="tpu_custom_call" | custom-call | tf_op jit(solution)/shard_map/pallas_call | solution.py:674
  29.0 0.6 %copy.8 = f32[2,8,8,128]{3,2,1,0:T(8,128)} copy(f32[2,8,8,128]{3,2,1,0:T(8,128)S(1)} %shard_map.64) | data formatting | bytes 131072

commit v5 on v4

--- a/solution.py
+++ b/solution.py
@@ -172,6 +172,8 @@
     ring,
     cco,
     cres,
+    zeros,
+    counted,
     sent,
     came,
 ):
@@ -219,40 +221,52 @@
             return -(-count // 8) * 8
         return 8 if dx != 0 and dy != 0 else 32
 
+    def halo_part(i, setup):
+        side = SIDES[i] if setup else PARTNERS[i]
+        halo = rows_of(side, setup)
+        if setup:
+            return pl.ds(0, halo + (24 if i >= 4 else 0))
+        return pl.ds(PAD - halo, halo + (16 if side[0] == 0 else 8))
+
+    def absent(side, dst, at):
+        @pl.when(jnp.logical_not(fits(*side)))
+        def _():
+            pltpu.make_async_copy(zeros.at[pl.ds(0, dst.shape[0])], dst, came.at[at]).start()
+
+    def wait_all(count, at):
+        part = counted.at[pl.ds(0, count)]
+        pltpu.make_async_copy(part, part, came.at[at]).wait()
+
     def setup_copy(i):
         dx, dy = SIDES[i]
-        part = pl.ds(0, rows_of((dx, dy), True) + (24 if i >= 4 else 0))
+        part = halo_part(i, True)
         at = PARTNERS.index((dx, dy))
         return pltpu.make_async_remote_copy(
-            ssend.at[i, part], srecv.at[i, part], sent.at[at], came.at[1, at], device_id=device(-dx, -dy), device_id_type=MESH
+            ssend.at[i, part], srecv.at[i, part], sent.at[at], came.at[0], device_id=device(-dx, -dy), device_id_type=MESH
         )
 
     def edge_copy(i):
         dx, dy = FAR[i]
         return pltpu.make_async_remote_copy(
-            xsend.at[0 if dx < 0 else 1], xrecv.at[i], sent.at[i], came.at[1, i], device_id=device(-dx, -dy), device_id_type=MESH
+            xsend.at[0 if dx < 0 else 1], xrecv.at[i], sent.at[i], came.at[1], device_id=device(-dx, -dy), device_id_type=MESH
         )
 
     def round_copy(i, k):
         dx, dy = PARTNERS[i]
-        halo = rows_of((dx, dy), False)
-        part = pl.ds(PAD - halo, halo + (16 if dx == 0 else 8))
+        part = halo_part(i, False)
         return pltpu.make_async_remote_copy(
-            rsend.at[k, i, part], rrecv.at[k, i, part], sent.at[i], came.at[lax.rem(k, 2), i], device_id=device(-dx, -dy), device_id_type=MESH
+            rsend.at[k, i, part], rrecv.at[k, i, part], sent.at[i], came.at[2 - 2 * lax.rem(k, 2)], device_id=device(-dx, -dy), device_id_type=MESH
         )
 
     def coef_copy(j):
         dx, dy = NEAR[j]
         at = PARTNERS.index((dx, dy)) if abs(dy) == 2 else N_PART + j - 2
         return pltpu.make_async_remote_copy(
-            ksend, krecv.at[j], sent.at[at], came.at[1, at], device_id=device(-dx, -dy), device_id_type=MESH
+            ksend, krecv.at[j], sent.at[at], came.at[1], device_id=device(-dx, -dy), device_id_type=MESH
         )
 
     def when_sent(side, act):
         pl.when(fits(-side[0], -side[1]))(act)
-
-    def when_there(side, act):
-        pl.when(fits(*side))(act)
 
     zero_rows = jnp.zeros((ROWS, LANES), jnp.float32)
     ext[MAT] = zero_rows - 1.0
@@ -281,6 +295,13 @@
     for i in range(4):
         when_sent(FAR[i], lambda: edge_copy(i).start())
 
+    zeros[...] = jnp.zeros((C_ROWS, LANES), jnp.float32)
+    for i, side in enumerate(SIDES):
+        absent(side, srecv.at[i, halo_part(i, True)], 0)
+    for i, side in enumerate(FAR[:4]):
+        absent(side, xrecv.at[i], 1)
+    for j, side in enumerate(NEAR):
+        absent(side, krecv.at[j], 1)
     mask[...] = zero_rows
     perm[...] = zero_rows
     poro[...] = zero_rows
@@ -365,33 +386,8 @@
     for j in range(4):
         when_sent(NEAR[j], lambda: coef_copy(j).start())
 
+    wait_all(sum(halo_part(i, True).size for i in range(8)), 0)
     for i, side in enumerate(SIDES):
-
-        @pl.when(jnp.logical_not(fits(*side)))
-        def _():
-            srecv[i] = jnp.zeros((80, LANES), jnp.float32)
-
-    for i, side in enumerate(PARTNERS):
-
-        @pl.when(jnp.logical_not(fits(*side)))
-        def _():
-            for k in range(ROUNDS):
-                rrecv[k, i] = jnp.zeros((R_ROWS, LANES), jnp.float32)
-
-    for j, side in enumerate(NEAR):
-
-        @pl.when(jnp.logical_not(fits(*side)))
-        def _():
-            krecv[j] = jnp.zeros((C_ROWS, LANES), jnp.float32)
-
-    for j, side in enumerate(FAR[:4]):
-
-        @pl.when(jnp.logical_not(fits(*side)))
-        def _():
-            xrecv[j] = jnp.zeros((24, LANES), jnp.float32)
-
-    for i, side in enumerate(SIDES):
-        when_there(side, lambda: setup_copy(i).wait_recv())
         unpack(side, True, srecv, (i,), ext, fits(*side))
     look_up_rows(0, ROWS, 32)
     face_rows(0, 144, 24)
@@ -517,12 +513,14 @@
             else:
                 rsend[k, i, pl.ds(PAD, 8), :] = beside
             when_sent(side, lambda: round_copy(i, k).start())
+        for i, side in enumerate(PARTNERS):
+            absent(side, rrecv.at[k, i, halo_part(i, False)], 2 - 2 * lax.rem(k, 2))
 
     def receive(k):
         for i, side in enumerate(PARTNERS):
             when_sent(side, lambda: round_copy(i, k).wait_send())
+        wait_all(sum(halo_part(i, False).size for i in range(N_PART)), 2 - 2 * lax.rem(k, 2))
         for i, side in enumerate(PARTNERS):
-            when_there(side, lambda: round_copy(i, k).wait_recv())
             if side not in FAR:
                 unpack(side, False, rrecv, (k, i), adj, None, PAD - rows_of(side, False))
         at_row = lax.broadcasted_iota(jnp.int32, (8, LANES), 0)
@@ -556,9 +554,7 @@
     for j, side in enumerate(NEAR):
         when_sent(side, lambda: coef_copy(j).wait_send())
         when_sent(FAR[j], lambda: edge_copy(j).wait_send())
-    for j in range(4):
-        when_there(NEAR[j], lambda: coef_copy(j).wait_recv())
-        when_there(FAR[j], lambda: edge_copy(j).wait_recv())
+    wait_all(4 * C_ROWS + 4 * 24, 1)
 
     def near(u):
         return NEAR.index((0, u))
@@ -708,8 +704,10 @@
                 tile(32),
                 tile(N_CBLK, 2, 8),
                 tile(4, 8),
+                tile(C_ROWS),
+                tile(4 * C_ROWS + 4 * 24),
                 dma((N_PART + 2,)),
-                dma((2, N_PART + 2)),
+                dma((3,)),
             ],
             compiler_params=pltpu.CompilerParams(
                 collective_id=0, has_side_effects=True, vmem_limit_bytes=32 * 1024 * 1024

time: 29.7 us -> 29.4 us (0.990)
  Pallas kernels: 29 us -> 28.6 us
    pallas_call x1, Pallas kernels: 29 us -> 28.6 us  [local(): pl.pallas_call(functools.partial(kernel, n_grp, n_sub), out_shape=pltpu.V...]
where the time goes in v5:
time: 29.4 us; the launch traced here: 29.3 us
  Pallas kernels  28.6 us (97%)
  local copies, waits for them, and re-layouts  0.63 us (2%)
    pallas_call x1, Pallas kernels, local(): pl.pallas_call(functools.partial(kernel, n_grp, n_sub), out_shape=pltpu.V...  28.6 us
    unnamed x1, local copies, waits for them, and re-layouts  0.63 us

profile of v5, /device:TPU:6, one launch (start us, length us, event | category | flops | bytes accessed | tf_op | source)
XLA Modules:
  0.0 29.3 jit_solution(11846556990266238953)
XLA Ops:
  0.0 28.6 %shard_map.64 = f32[2,8,8,128]{3,2,1,0:T(8,128)S(1)} custom-call(f32[2,8,8,128]{3,2,1,0:T(8,128)} %cot_hbm.1, f32[8,8,128]{2,1,0:T(8,128)} %head_hbm.1, s32[8,8,128]{2,1,0:T(8,128)} %mat_hbm.1, s32[3,8,8,128]{3,2,1,0:T(8,128)} %flag_hbm.1, f32[8]{0:T(128)} %perm_hbm.1, f32[8]{0:T(128)} %poro_hbm.1), custom_call_target="tpu_custom_call" | custom-call | tf_op jit(solution)/shard_map/pallas_call | solution.py:670
  28.6 0.6 %copy.8 = f32[2,8,8,128]{3,2,1,0:T(8,128)} copy(f32[2,8,8,128]{3,2,1,0:T(8,128)S(1)} %shard_map.64) | data formatting | bytes 131072

commit v6 on v5

--- a/solution.py
+++ b/solution.py
@@ -121,13 +121,10 @@
     out = []
     for f, first in ((0, TX), (1, SX)):
         mid = field[f, here, :]
-        total = co[first, here, :] * field[f, pl.ds(lo + PITCH, n), :]
-        total = total + co[first + 1, here, :] * field[f, pl.ds(lo - PITCH, n), :]
-        total = total + co[first + 2, here, :] * field[f, pl.ds(lo + 1, n), :]
-        total = total + co[first + 3, here, :] * field[f, pl.ds(lo - 1, n), :]
-        total = total + co[first + 4, here, :] * next_lane(mid)
-        total = total + co[first + 5, here, :] * last_lane(mid)
-        out += [mid, total]
+        one = co[first, here, :] * field[f, pl.ds(lo + PITCH, n), :] + co[first + 1, here, :] * field[f, pl.ds(lo - PITCH, n), :]
+        two = co[first + 2, here, :] * field[f, pl.ds(lo + 1, n), :] + co[first + 3, here, :] * field[f, pl.ds(lo - 1, n), :]
+        three = co[first + 4, here, :] * next_lane(mid) + co[first + 5, here, :] * last_lane(mid)
+        out += [mid, (one + two) + three]
     return out
 
 
@@ -172,6 +169,8 @@
     ring,
     cco,
     cres,
+    wt,
+    wx,
     zeros,
     counted,
     sent,
@@ -272,6 +271,10 @@
     ext[MAT] = zero_rows - 1.0
     for f in range(1, 7):
         ext[f] = zero_rows
+    perm[...] = zero_rows
+    poro[...] = zero_rows
+    for m in range(9):
+        face[m, pl.ds(0, 32), :] = jnp.zeros((32, LANES), jnp.float32)
     for load in loads:
         load.wait()
     for x in range(8):
@@ -288,32 +291,6 @@
         pack(side, True, ext, ssend, (i,))
         if i >= 4:
             ssend[i, pl.ds(24, 24), :] = xsend[0 if side[0] < 0 else 1]
-
-    pl.semaphore_wait(barrier, expected)
-    for i in reversed(range(8)):
-        when_sent(SIDES[i], lambda: setup_copy(i).start())
-    for i in range(4):
-        when_sent(FAR[i], lambda: edge_copy(i).start())
-
-    zeros[...] = jnp.zeros((C_ROWS, LANES), jnp.float32)
-    for i, side in enumerate(SIDES):
-        absent(side, srecv.at[i, halo_part(i, True)], 0)
-    for i, side in enumerate(FAR[:4]):
-        absent(side, xrecv.at[i], 1)
-    for j, side in enumerate(NEAR):
-        absent(side, krecv.at[j], 1)
-    mask[...] = zero_rows
-    perm[...] = zero_rows
-    poro[...] = zero_rows
-    for f in range(2):
-        adj[f] = zero_rows
-        inc[f] = zero_rows
-        grd[f] = zero_rows
-        mid[f] = zero_rows
-    for m in range(9):
-        face[m, pl.ds(0, 32), :] = jnp.zeros((32, LANES), jnp.float32)
-    for x in range(-1, 9):
-        mask[rows(x, -1, 10), :] = jnp.ones((10, LANES), jnp.float32)
 
     def look_up(mats):
         perm_here = jnp.zeros_like(mats)
@@ -383,8 +360,30 @@
     ]
     for slot, (field, where) in enumerate(raw):
         ksend[pl.ds(C_RAW + 8 * slot, 8), :] = ext[field, where, :]
+    pl.semaphore_wait(barrier, expected)
+    for i in reversed(range(8)):
+        when_sent(SIDES[i], lambda: setup_copy(i).start())
+    for i in range(4):
+        when_sent(FAR[i], lambda: edge_copy(i).start())
+
     for j in range(4):
         when_sent(NEAR[j], lambda: coef_copy(j).start())
+
+    zeros[...] = jnp.zeros((C_ROWS, LANES), jnp.float32)
+    for i, side in enumerate(SIDES):
+        absent(side, srecv.at[i, halo_part(i, True)], 0)
+    for i, side in enumerate(FAR[:4]):
+        absent(side, xrecv.at[i], 1)
+    for j, side in enumerate(NEAR):
+        absent(side, krecv.at[j], 1)
+    mask[...] = zero_rows
+    for f in range(2):
+        adj[f] = zero_rows
+        grd[f] = zero_rows
+        mid[f] = zero_rows
+    for x in range(-1, 9):
+        mask[rows(x, -1, 10), :] = jnp.ones((10, LANES), jnp.float32)
+
 
     wait_all(sum(halo_part(i, True).size for i in range(8)), 0)
     for i, side in enumerate(SIDES):
@@ -472,36 +471,35 @@
                 here = rows(x, 0)
                 more = THETA * (fin[f, here, :] + grown[f][x // 4])
                 new = adj[f, here, :] + more
-                inc[f, here, :] = more
+                inc[f, x] = more
                 adj[f, here, :] = new
                 out_ref[f, x] = new
 
     def send(k):
-        for lo in range(16, 144, 16):
-            here = pl.ds(lo, 16)
-            z_p, s_p, z_c, s_c = couple(co, inc, lo, 16)
-            res[0, here, :] = co[BPP, here, :] * z_p + co[BPC, here, :] * z_c - s_p
-            res[1, here, :] = co[BCP, here, :] * z_p + co[BCC, here, :] * z_c - s_c
-
         def place(at, value):
             ring[pl.ds(8 + at, 1), :] = value
 
+        e = [[inc[f, x] for x in range(8)] for f in range(2)]
         for f in range(2):
             for cx in range(2):
-                total = res[f, rows(4 * cx, 0), :]
-                for x in range(4 * cx + 1, 4 * cx + 4):
-                    total = total + res[f, rows(x, 0), :]
-                total = four_sum(total)
-                place(8 * f + 4 * cx + 1, total[0:1])
-                place(8 * f + 4 * cx + 2, total[4:5])
-            for at, y in ((0, -1), (3, 8)):
-                total = four_sum(res[f, column(y), :])
-                place(8 * f + at, total[0:1])
-                place(8 * f + 4 + at, total[4:5])
-            for at, x in ((16, -1), (20, 8)):
-                total = four_sum(res[f, rows(x, 0), :])
-                place(at + 2 * f, total[0:1])
-                place(at + 2 * f + 1, total[4:5])
+                terms = [[], [], [], [], []]
+                for x in range(4 * cx, 4 * cx + 4):
+                    terms[0].append(wt[6 * f, x] * e[f][x] + wt[6 * f + 1, x] * e[1 - f][x])
+                    for m in range(4):
+                        terms[1 + m].append(wt[6 * f + 2 + m, x] * e[f][x])
+                total, y_next, y_last, z_next, z_last = ((t[0] + t[1]) + (t[2] + t[3]) for t in terms)
+                total = total - (last_lane(z_next) + next_lane(z_last))
+                other = wx[f, 1, 0] * e[f][4] if cx == 0 else wx[f, 0, 1] * e[f][3]
+                total = four_sum(total - other)
+                at = 8 * f + 4 * cx
+                place(at, -y_last[0:1])
+                place(at + 1, total[0:1] - y_last[4:5])
+                place(at + 2, total[4:5] - y_next[3:4])
+                place(at + 3, -y_next[7:8])
+            for at, value in ((16, wx[f, 0, 0] * e[f][0]), (20, wx[f, 1, 1] * e[f][7])):
+                total = four_sum(value)
+                place(at + 2 * f, -total[0:1])
+                place(at + 2 * f + 1, -total[4:5])
         sums = lane_sum(ring[pl.ds(8, 24), :])
         ring[pl.ds(8, 24), :] = sums
         along, beside = sums[0:16], sums[16:24]
@@ -644,6 +642,31 @@
             DISP * m_t + (m_a if cx == 0 else m_b),
         )):
             cco[b, cx] = value
+    y_at = lax.broadcasted_iota(jnp.int32, (8, LANES), 0) % AGG
+    z_at = lax.broadcasted_iota(jnp.int32, (8, LANES), 1) % AGG
+    for x in range(8):
+        here = rows(x, 0)
+        to_next = [[co[TX + 2 * d, here, :] for d in range(3)], [DISP * face[3 * d, here, :] + face[3 * d + 2, here, :] for d in range(3)]]
+        to_last = [
+            [co[TXM + 2 * d, here, :] for d in range(3)],
+            [co[SX, rows(x - 1, 0), :], co[SY, rows(x, -1), :], last_lane(co[SZ, here, :])],
+        ]
+        for f in range(2):
+            own = co[BCC if f else BPP, here, :]
+            if x % AGG != AGG - 1:
+                own = own - to_next[f][0]
+            if x % AGG != 0:
+                own = own - to_last[f][0]
+            y_next, y_last = (jnp.where(y_at == edge, v[f][1], 0.0) for edge, v in ((AGG - 1, to_next), (0, to_last)))
+            z_next, z_last = (jnp.where(z_at == edge, v[f][2], 0.0) for edge, v in ((AGG - 1, to_next), (0, to_last)))
+            own = own - (((to_next[f][1] - y_next) + (to_last[f][1] - y_last)) + ((to_next[f][2] - z_next) + (to_last[f][2] - z_last)))
+            for m, value in enumerate((own, co[BCP if f else BPC, here, :], y_next, y_last, z_next, z_last)):
+                wt[6 * f + m, x] = value
+            if x % AGG == 0:
+                wx[f, x // AGG, 0] = to_last[f][0]
+            if x % AGG == AGG - 1:
+                wx[f, x // AGG, 1] = to_next[f][0]
+
     update()
     send(0)
 
@@ -686,7 +709,7 @@
                 tile(9, ROWS),
                 tile(N_COEF, ROWS),
                 tile(2, ROWS),
-                tile(2, ROWS),
+                tile(2, 8, 8),
                 tile(2, ROWS),
                 tile(2, ROWS),
                 tile(2, ROWS),
@@ -704,6 +727,8 @@
                 tile(32),
                 tile(N_CBLK, 2, 8),
                 tile(4, 8),
+                tile(12, 8, 8),
+                tile(2, 2, 2, 8),
                 tile(C_ROWS),
                 tile(4 * C_ROWS + 4 * 24),
                 dma((N_PART + 2,)),

time: 29.4 us -> 29.2 us (level)
  no operation moved by 1% of the time
where the time goes in v6:
time: 29.2 us; the launch traced here: 29.1 us
  Pallas kernels  28.4 us (97%)
  local copies, waits for them, and re-layouts  0.63 us (2%)
    pallas_call x1, Pallas kernels, local(): pl.pallas_call(functools.partial(kernel, n_grp, n_sub), out_shape=pltpu.V...  28.4 us
    unnamed x1, local copies, waits for them, and re-layouts  0.63 us

profile of v6, /device:TPU:6, one launch (start us, length us, event | category | flops | bytes accessed | tf_op | source)
XLA Modules:
  0.0 29.1 jit_solution(15430964160589161595)
XLA Ops:
  0.0 28.4 %shard_map.64 = f32[2,8,8,128]{3,2,1,0:T(8,128)S(1)} custom-call(f32[2,8,8,128]{3,2,1,0:T(8,128)} %cot_hbm.1, f32[8,8,128]{2,1,0:T(8,128)} %head_hbm.1, s32[8,8,128]{2,1,0:T(8,128)} %mat_hbm.1, s32[3,8,8,128]{3,2,1,0:T(8,128)} %flag_hbm.1, f32[8]{0:T(128)} %perm_hbm.1, f32[8]{0:T(128)} %poro_hbm.1), custom_call_target="tpu_custom_call" | custom-call | tf_op jit(solution)/shard_map/pallas_call | solution.py:693
  28.4 0.6 %copy.8 = f32[2,8,8,128]{3,2,1,0:T(8,128)} copy(f32[2,8,8,128]{3,2,1,0:T(8,128)S(1)} %shard_map.64) | data formatting | bytes 131072

commit v7 on v6

--- a/solution.py
+++ b/solution.py
@@ -106,14 +106,15 @@
 
 
 def lane_sum(value):
-    lane = lax.broadcasted_iota(jnp.int32, value.shape, 1)
-    total = value + jnp.where(lane % 2 == 0, next_lane(value), last_lane(value))
-    return total + jnp.where(lane % AGG < 2, next_lane(total, 2), last_lane(total, 2))
+    at = lax.broadcasted_iota(jnp.int32, value.shape, 1) % AGG
+    one = jnp.where(at < 3, next_lane(value), last_lane(value, 3))
+    two = jnp.where(at < 2, next_lane(value, 2), last_lane(value, 2))
+    three = jnp.where(at < 1, next_lane(value, 3), last_lane(value))
+    return (value + one) + (two + three)
 
 
 def four_sum(value):
-    total = value + pltpu.roll(value, 7, 0)
-    return total + pltpu.roll(total, 6, 0)
+    return (value + pltpu.roll(value, 7, 0)) + (pltpu.roll(value, 6, 0) + pltpu.roll(value, 5, 0))
 
 
 def couple(co, field, lo, n):

time: 29.2 us -> 28.9 us (0.990)
  no operation moved by 1% of the time
where the time goes in v7:
time: 28.9 us; the launch traced here: 28.8 us
  Pallas kernels  28.2 us (98%)
  local copies, waits for them, and re-layouts  0.63 us (2%)
    pallas_call x1, Pallas kernels, local(): pl.pallas_call(functools.partial(kernel, n_grp, n_sub), out_shape=pltpu.V...  28.2 us
    unnamed x1, local copies, waits for them, and re-layouts  0.63 us

profile of v7, /device:TPU:6, one launch (start us, length us, event | category | flops | bytes accessed | tf_op | source)
XLA Modules:
  0.0 28.8 jit_solution(15175334527854602333)
XLA Ops:
  0.0 28.2 %shard_map.64 = f32[2,8,8,128]{3,2,1,0:T(8,128)S(1)} custom-call(f32[2,8,8,128]{3,2,1,0:T(8,128)} %cot_hbm.1, f32[8,8,128]{2,1,0:T(8,128)} %head_hbm.1, s32[8,8,128]{2,1,0:T(8,128)} %mat_hbm.1, s32[3,8,8,128]{3,2,1,0:T(8,128)} %flag_hbm.1, f32[8]{0:T(128)} %perm_hbm.1, f32[8]{0:T(128)} %poro_hbm.1), custom_call_target="tpu_custom_call" | custom-call | tf_op jit(solution)/shard_map/pallas_call | solution.py:694
  28.2 0.6 %copy.8 = f32[2,8,8,128]{3,2,1,0:T(8,128)} copy(f32[2,8,8,128]{3,2,1,0:T(8,128)S(1)} %shard_map.64) | data formatting | bytes 131072

commit v8 on v7

--- a/solution.py
+++ b/solution.py
@@ -111,6 +111,13 @@
     two = jnp.where(at < 2, next_lane(value, 2), last_lane(value, 2))
     three = jnp.where(at < 1, next_lane(value, 3), last_lane(value))
     return (value + one) + (two + three)
+
+
+def lane_pass(value):
+    at = lax.broadcasted_iota(jnp.int32, value.shape, 1) % AGG
+    back = jnp.where(at < 2, jnp.where(at < 1, last_lane(value), last_lane(value, 2)), jnp.where(at < 3, last_lane(value, 3), last_lane(value, 4)))
+    ahead = jnp.where(at < 2, jnp.where(at < 1, next_lane(value, 4), next_lane(value, 3)), jnp.where(at < 3, next_lane(value, 2), next_lane(value)))
+    return back + ahead
 
 
 def four_sum(value):
@@ -168,6 +175,7 @@
     cin,
     cedge,
     ring,
+    zring,
     cco,
     cres,
     wt,
@@ -377,6 +385,7 @@
         absent(side, xrecv.at[i], 1)
     for j, side in enumerate(NEAR):
         absent(side, krecv.at[j], 1)
+    zring[...] = jnp.zeros((16, LANES), jnp.float32)
     mask[...] = zero_rows
     for f in range(2):
         adj[f] = zero_rows
@@ -489,7 +498,9 @@
                     for m in range(4):
                         terms[1 + m].append(wt[6 * f + 2 + m, x] * e[f][x])
                 total, y_next, y_last, z_next, z_last = ((t[0] + t[1]) + (t[2] + t[3]) for t in terms)
-                total = total - (last_lane(z_next) + next_lane(z_last))
+                passed = four_sum(z_next + z_last)
+                zring[pl.ds(8 * f + 4 * cx + 1, 1), :] = passed[0:1]
+                zring[pl.ds(8 * f + 4 * cx + 2, 1), :] = passed[4:5]
                 other = wx[f, 1, 0] * e[f][4] if cx == 0 else wx[f, 0, 1] * e[f][3]
                 total = four_sum(total - other)
                 at = 8 * f + 4 * cx
@@ -501,9 +512,9 @@
                 total = four_sum(value)
                 place(at + 2 * f, -total[0:1])
                 place(at + 2 * f + 1, -total[4:5])
-        sums = lane_sum(ring[pl.ds(8, 24), :])
-        ring[pl.ds(8, 24), :] = sums
-        along, beside = sums[0:16], sums[16:24]
+        along = lane_sum(ring[pl.ds(8, 16), :]) - lane_pass(zring[...])
+        beside = lane_sum(ring[pl.ds(24, 8), :])
+        ring[pl.ds(8, 16), :] = along
         for i, side in enumerate(PARTNERS):
             if side not in FAR:
                 pack(side, False, adj, rsend, (k, i), PAD - rows_of(side, False))
@@ -726,6 +737,7 @@
                 tile(13, 8),
                 tile(10, 8),
                 tile(32),
+                tile(16),
                 tile(N_CBLK, 2, 8),
                 tile(4, 8),
                 tile(12, 8, 8),

time: 28.9 us -> 28.9 us (level)
  no operation moved by 1% of the time
where the time goes in v8:
time: 28.9 us; the launch traced here: 28.8 us
  Pallas kernels  28.1 us (97%)
  local copies, waits for them, and re-layouts  0.63 us (2%)
    pallas_call x1, Pallas kernels, local(): pl.pallas_call(functools.partial(kernel, n_grp, n_sub), out_shape=pltpu.V...  28.1 us
    unnamed x1, local copies, waits for them, and re-layouts  0.63 us

profile of v8, /device:TPU:6, one launch (start us, length us, event | category | flops | bytes accessed | tf_op | source)
XLA Modules:
  0.0 28.8 jit_solution(3367866304300186016)
XLA Ops:
  0.0 28.1 %shard_map.64 = f32[2,8,8,128]{3,2,1,0:T(8,128)S(1)} custom-call(f32[2,8,8,128]{3,2,1,0:T(8,128)} %cot_hbm.1, f32[8,8,128]{2,1,0:T(8,128)} %head_hbm.1, s32[8,8,128]{2,1,0:T(8,128)} %mat_hbm.1, s32[3,8,8,128]{3,2,1,0:T(8,128)} %flag_hbm.1, f32[8]{0:T(128)} %perm_hbm.1, f32[8]{0:T(128)} %poro_hbm.1), custom_call_target="tpu_custom_call" | custom-call | tf_op jit(solution)/shard_map/pallas_call | solution.py:705
  28.1 0.6 %copy.8 = f32[2,8,8,128]{3,2,1,0:T(8,128)} copy(f32[2,8,8,128]{3,2,1,0:T(8,128)S(1)} %shard_map.64) | data formatting | bytes 131072

commit v9 on v8

--- a/solution.py
+++ b/solution.py
@@ -530,9 +530,6 @@
         for i, side in enumerate(PARTNERS):
             when_sent(side, lambda: round_copy(i, k).wait_send())
         wait_all(sum(halo_part(i, False).size for i in range(N_PART)), 2 - 2 * lax.rem(k, 2))
-        for i, side in enumerate(PARTNERS):
-            if side not in FAR:
-                unpack(side, False, rrecv, (k, i), adj, None, PAD - rows_of(side, False))
         at_row = lax.broadcasted_iota(jnp.int32, (8, LANES), 0)
         for f in range(2):
             for cx in range(2):
@@ -551,6 +548,9 @@
                 three = jnp.where(at_row < 1, beside(-2), jnp.where(at_row < 3, beside(-1), beside(0)))
                 three = jnp.where(at_row < 5, three, jnp.where(at_row < 7, beside(1), beside(2)))
                 cres[item] = cres[item] - ((one + two) + three)
+        for i, side in enumerate(PARTNERS):
+            if side not in FAR:
+                unpack(side, False, rrecv, (k, i), adj, None, PAD - rows_of(side, False))
         for lo in range(16, 144, 16):
             here = pl.ds(lo, 16)
             z_p, s_p, z_c, s_c = couple(co, adj, lo, 16)

time: 28.9 us -> 28.9 us (level)
  no operation moved by 1% of the time
where the time goes in v9:
time: 28.9 us; the launch traced here: 28.8 us
  Pallas kernels  28.1 us (97%)
  local copies, waits for them, and re-layouts  0.63 us (2%)
    pallas_call x1, Pallas kernels, local(): pl.pallas_call(functools.partial(kernel, n_grp, n_sub), out_shape=pltpu.V...  28.1 us
    unnamed x1, local copies, waits for them, and re-layouts  0.63 us

profile of v9, /device:TPU:6, one launch (start us, length us, event | category | flops | bytes accessed | tf_op | source)
XLA Modules:
  0.0 28.8 jit_solution(12365907772734982756)
XLA Ops:
  0.0 28.1 %shard_map.64 = f32[2,8,8,128]{3,2,1,0:T(8,128)S(1)} custom-call(f32[2,8,8,128]{3,2,1,0:T(8,128)} %cot_hbm.1, f32[8,8,128]{2,1,0:T(8,128)} %head_hbm.1, s32[8,8,128]{2,1,0:T(8,128)} %mat_hbm.1, s32[3,8,8,128]{3,2,1,0:T(8,128)} %flag_hbm.1, f32[8]{0:T(128)} %perm_hbm.1, f32[8]{0:T(128)} %poro_hbm.1), custom_call_target="tpu_custom_call" | custom-call | tf_op jit(solution)/shard_map/pallas_call | solution.py:705
  28.1 0.6 %copy.8 = f32[2,8,8,128]{3,2,1,0:T(8,128)} copy(f32[2,8,8,128]{3,2,1,0:T(8,128)S(1)} %shard_map.64) | data formatting | bytes 131072
